TPU v7x, 128 devices: a whole 4x4x4 slice. The times are simulated.
128 devices in a mesh: rep: 32 (over x, z_hi, y), shard: 4 (over z_lo, core).
Axes of the slice: x: 4, y: 4, z: 4 (z_hi: 2, z_lo: 2; z = z_hi * 2 + z_lo), core: 2. Of those that a mesh axis runs over, the one named last changes fastest.
Arguments:
- inputs: bfloat16 [16384, 1024], P(('rep', 'shard')), may hold values from -10 to 10
- lengths: int32 [32], P('rep'), may hold values from 385 to 512, as said below
- gains: bfloat16 [2, 1024], P(None, 'shard'), may hold values from 0.5 to 1.5
- shifts: bfloat16 [2, 1024], P(None, 'shard'), may hold values from -4 to 4
- triple: bfloat16 [2, 1024, 3072], P(None, 'shard'), may hold values from -0.1875 to 0.1875
- triple_bias: bfloat16 [2, 3072], P(None, 'shard'), may hold values from -4 to 4
- merger: bfloat16 [2, 1024, 1024], P(None, 'shard'), may hold values from -1.5 to 1.5
- merger_bias: bfloat16 [2, 1024], P(None, 'shard'), may hold values from -4 to 4
- expander: bfloat16 [2, 1024, 4096], P(None, 'shard'), may hold values from -0.1875 to 0.1875
- expander_bias: bfloat16 [2, 4096], P(None, 'shard'), may hold values from -4 to 4
- shrinker: bfloat16 [2, 4096, 1024], P(None, 'shard'), may hold values from -0.09375 to 0.09375
- shrinker_bias: bfloat16 [2, 1024], P(None, 'shard'), may hold values from -4 to 4
- cotangent: bfloat16 [16384, 1024], P(('rep', 'shard')), may hold values from -6 to 6
Outputs:
- hidden_out: bfloat16 [16384, 1024], P(('rep', 'shard'))
- input_grad: float32 [16384, 1024], P(('rep', 'shard'))
- gains_gradient: float32 [2, 1024], P(None, 'shard')
- shifts_gradient: float32 [2, 1024], P(None, 'shard')
- triple_gradient: float32 [2, 1024, 3072], P(None, 'shard')
- triple_bias_gradient: float32 [2, 3072], P(None, 'shard')
- merger_gradient: float32 [2, 1024, 1024], P(None, 'shard')
- merger_bias_gradient: float32 [2, 1024], P(None, 'shard')
- expander_gradient: float32 [2, 1024, 4096], P(None, 'shard')
- expander_bias_gradient: float32 [2, 4096], P(None, 'shard')
- shrinker_gradient: float32 [2, 4096, 1024], P(None, 'shard')
- shrinker_bias_gradient: float32 [2, 1024], P(None, 'shard')
- rms_stats: float32 [32, 6], P('rep')
Inputs may be any that keep to these rules, and one draw needn't show every extreme that they name: `lengths`: one sequence of every draw has all 512 slots valid.
All inputs are finite; a program needn't handle non-finite values.
Results may differ from a plain program's by a relative error of at most 0.025.
Values may be sent and summed in bfloat16 or wider, within the bound.
No kernel may reach another device: no remote copies, remote signals or barrier semaphores. Data moves between devices by JAX's collectives and lax.ppermute only.
A program may use at most 256 MiB of HBM per device.

v0:
```python
import math

import jax
import jax.numpy as jnp
from jax import lax
from jax.sharding import PartitionSpec as P

HD = 64
ROT = 32
LAYERS = 2


EPS_NORM = 1e-05


def layer_norm(state, gain, shift):
    mean = jnp.mean(state, axis=-1, keepdims=True)
    centred = state - mean
    spread = jnp.mean(centred * centred, axis=-1, keepdims=True)
    return centred * lax.rsqrt(spread + EPS_NORM) * gain + shift


def angles(positions):
    index = jnp.arange(ROT // 2, dtype=jnp.float32)
    freq = jnp.exp(index * (-2.0 * math.log(10000.0) / ROT))
    phase = positions[:, None] * freq[None, :]
    return (jnp.cos(phase)[:, None, :], jnp.sin(phase)[:, None, :])


def rotate(values, cosine, sine):
    half = ROT // 2
    first = values[..., :half]
    second = values[..., half:ROT]
    return jnp.concatenate(
        [first * cosine - second * sine, second * cosine + first * sine, values[..., ROT:]], axis=-1
    )


def gelu_tanh(values):
    return jax.nn.gelu(values, approximate=True)


def body(
    inputs,
    lengths,
    gains,
    shifts,
    triple,
    triple_bias,
    merger,
    merger_bias,
    expander,
    expander_bias,
    shrinker,
    shrinker_bias,
    cotangent,
):
    rows = inputs.shape[0]
    width = inputs.shape[1]
    heads = width // HD
    shards = lax.axis_size("shard")
    seq_len = rows * shards
    first_row = lax.axis_index("shard") * rows
    length = lengths[0]
    positions = first_row + jnp.arange(rows, dtype=jnp.int32)
    valid = (positions < length).astype(jnp.float32)
    key_pos = jnp.arange(seq_len, dtype=jnp.int32)
    allowed = (key_pos[None, :] <= positions[:, None]) & (key_pos[None, :] < length)
    cosine, sine = angles(positions.astype(jnp.float32))
    scale = HD ** (-0.5)
    state = inputs.astype(jnp.float32)
    saved = []
    squares = []
    for layer in range(LAYERS):
        weights = (
            lax.all_gather(gains[layer], "shard", axis=0, tiled=True),
            lax.all_gather(shifts[layer], "shard", axis=0, tiled=True),
            lax.all_gather(triple[layer], "shard", axis=0, tiled=True),
            lax.all_gather(triple_bias[layer], "shard", axis=0, tiled=True),
            lax.all_gather(merger[layer], "shard", axis=0, tiled=True),
            lax.all_gather(merger_bias[layer], "shard", axis=0, tiled=True),
            lax.all_gather(expander[layer], "shard", axis=0, tiled=True),
            lax.all_gather(expander_bias[layer], "shard", axis=0, tiled=True),
            lax.all_gather(shrinker[layer], "shard", axis=0, tiled=True),
            lax.all_gather(shrinker_bias[layer], "shard", axis=0, tiled=True),
        )
        (
            gain_full,
            shift_full,
            triple_full,
            triple_add,
            merger_full,
            merger_add,
            expander_full,
            expander_add,
            shrinker_full,
            shrinker_add,
        ) = weights
        normed = layer_norm(
            state, gain_full.astype(jnp.float32), shift_full.astype(jnp.float32)
        ).astype(jnp.bfloat16)
        triple_out = jnp.dot(
            normed, triple_full, preferred_element_type=jnp.float32
        ) + triple_add.astype(jnp.float32)
        query = (
            rotate(triple_out[:, :width].reshape(rows, heads, HD), cosine, sine) * scale
        ).astype(jnp.bfloat16)
        key_local = (
            rotate(triple_out[:, width : 2 * width].reshape(rows, heads, HD), cosine, sine)
            .astype(jnp.bfloat16)
            .reshape(rows, width)
        )
        value_local = triple_out[:, 2 * width :].astype(jnp.bfloat16)
        keys_all, values_all = (
            lax.all_gather(key_local, "shard", axis=0, tiled=True),
            lax.all_gather(value_local, "shard", axis=0, tiled=True),
        )
        scores = jnp.einsum(
            "qhd,khd->hqk",
            query,
            keys_all.reshape(seq_len, heads, HD),
            preferred_element_type=jnp.float32,
        )
        scores = jnp.where(allowed[None], scores, -1000000000.0)
        peak = jnp.max(scores, axis=-1, keepdims=True)
        powered = jnp.exp(scores - peak)
        total = jnp.sum(powered, axis=-1, keepdims=True)
        probs_low = (powered / total).astype(jnp.bfloat16)
        log_total = peak + jnp.log(total)
        mixed = jnp.einsum(
            "hqk,khd->qhd",
            probs_low,
            values_all.reshape(seq_len, heads, HD),
            preferred_element_type=jnp.float32,
        )
        mixed = mixed.astype(jnp.bfloat16).reshape(rows, width)
        attended = jnp.dot(
            mixed, merger_full, preferred_element_type=jnp.float32
        ) + merger_add.astype(jnp.float32)
        before = jnp.dot(
            normed, expander_full, preferred_element_type=jnp.float32
        ) + expander_add.astype(jnp.float32)
        activated = gelu_tanh(before).astype(jnp.bfloat16)
        branch = jnp.dot(
            activated, shrinker_full, preferred_element_type=jnp.float32
        ) + shrinker_add.astype(jnp.float32)
        for item in (state, attended, branch):
            squares.append(jnp.sum(jnp.sum(item * item, axis=1) * valid))
        stored = (key_local, value_local)
        saved.append((state, normed, query, log_total, mixed, before, activated, stored))
        state = state + attended + branch
    totals = lax.psum(jnp.stack(squares), "shard")
    rms_stats = jnp.sqrt(totals / (length.astype(jnp.float32) * width) + 1e-06)[None, :]
    hidden_out = (state * valid[:, None]).astype(jnp.bfloat16)
    slope = cotangent.astype(jnp.float32) * valid[:, None]
    collected = [None] * LAYERS
    for layer in reversed(range(LAYERS)):
        state_in, normed, query, log_total, mixed, before, activated, stored = saved[layer]
        key_local, value_local = stored
        weights = (
            lax.all_gather(gains[layer], "shard", axis=0, tiled=True),
            lax.all_gather(shifts[layer], "shard", axis=0, tiled=True),
            lax.all_gather(triple[layer], "shard", axis=0, tiled=True),
            lax.all_gather(triple_bias[layer], "shard", axis=0, tiled=True),
            lax.all_gather(merger[layer], "shard", axis=0, tiled=True),
            lax.all_gather(merger_bias[layer], "shard", axis=0, tiled=True),
            lax.all_gather(expander[layer], "shard", axis=0, tiled=True),
            lax.all_gather(expander_bias[layer], "shard", axis=0, tiled=True),
            lax.all_gather(shrinker[layer], "shard", axis=0, tiled=True),
            lax.all_gather(shrinker_bias[layer], "shard", axis=0, tiled=True),
        )
        keys_all, values_all = (
            lax.all_gather(key_local, "shard", axis=0, tiled=True),
            lax.all_gather(value_local, "shard", axis=0, tiled=True),
        )
        (
            gain_full,
            shift_full,
            triple_full,
            triple_add,
            merger_full,
            merger_add,
            expander_full,
            expander_add,
            shrinker_full,
            shrinker_add,
        ) = weights
        upstream = slope.astype(jnp.bfloat16)
        bias_slope = jnp.sum(upstream.astype(jnp.float32), axis=0)
        shrinker_slope = jnp.dot(activated.T, upstream, preferred_element_type=jnp.float32)
        merger_slope = jnp.dot(mixed.T, upstream, preferred_element_type=jnp.float32)
        slope_activated = jnp.dot(upstream, shrinker_full.T, preferred_element_type=jnp.float32)
        ignored, gelu_pull = jax.vjp(gelu_tanh, before)
        slope_before = gelu_pull(slope_activated)[0].astype(jnp.bfloat16)
        expander_add_slope = jnp.sum(slope_before.astype(jnp.float32), axis=0)
        expander_slope = jnp.dot(normed.T, slope_before, preferred_element_type=jnp.float32)
        slope_normed = jnp.dot(slope_before, expander_full.T, preferred_element_type=jnp.float32)
        slope_mixed = (
            jnp.dot(upstream, merger_full.T, preferred_element_type=jnp.float32)
            .astype(jnp.bfloat16)
            .reshape(rows, heads, HD)
        )
        keys_three = keys_all.reshape(seq_len, heads, HD)
        values_three = values_all.reshape(seq_len, heads, HD)
        scores = jnp.einsum("qhd,khd->hqk", query, keys_three, preferred_element_type=jnp.float32)
        probs = jnp.where(allowed[None], jnp.exp(scores - log_total), 0.0)
        slope_probs = jnp.einsum(
            "qhd,khd->hqk", slope_mixed, values_three, preferred_element_type=jnp.float32
        )
        centre = jnp.sum(probs * slope_probs, axis=-1, keepdims=True)
        slope_scores = (probs * (slope_probs - centre)).astype(jnp.bfloat16)
        slope_query = jnp.einsum(
            "hqk,khd->qhd", slope_scores, keys_three, preferred_element_type=jnp.float32
        )
        key_part = jnp.einsum(
            "hqk,qhd->khd", slope_scores, query, preferred_element_type=jnp.float32
        ).reshape(seq_len, width)
        value_part = jnp.einsum(
            "hqk,qhd->khd",
            probs.astype(jnp.bfloat16),
            slope_mixed,
            preferred_element_type=jnp.float32,
        ).reshape(seq_len, width)
        slope_keys, slope_values = (
            lax.psum_scatter(
                key_part.astype(jnp.bfloat16), "shard", scatter_dimension=0, tiled=True
            ).astype(jnp.float32),
            lax.psum_scatter(
                value_part.astype(jnp.bfloat16), "shard", scatter_dimension=0, tiled=True
            ).astype(jnp.float32),
        )
        slope_triple = jnp.concatenate(
            [
                rotate(slope_query, cosine, -sine).reshape(rows, width) * scale,
                rotate(slope_keys.reshape(rows, heads, HD), cosine, -sine).reshape(rows, width),
                slope_values,
            ],
            axis=1,
        ).astype(jnp.bfloat16)
        triple_add_slope = jnp.sum(slope_triple.astype(jnp.float32), axis=0)
        triple_slope = jnp.dot(normed.T, slope_triple, preferred_element_type=jnp.float32)
        slope_normed = slope_normed + jnp.dot(
            slope_triple, triple_full.T, preferred_element_type=jnp.float32
        )
        ignored, norm_pull = jax.vjp(
            layer_norm, state_in, gain_full.astype(jnp.float32), shift_full.astype(jnp.float32)
        )
        slope_state, gain_slope, shift_slope = norm_pull(slope_normed)
        slope = slope + slope_state
        owned = (
            lax.psum_scatter(
                gain_slope.astype(jnp.bfloat16), "shard", scatter_dimension=0, tiled=True
            ).astype(jnp.float32),
            lax.psum_scatter(
                shift_slope.astype(jnp.bfloat16), "shard", scatter_dimension=0, tiled=True
            ).astype(jnp.float32),
            lax.psum_scatter(
                triple_slope.astype(jnp.bfloat16), "shard", scatter_dimension=0, tiled=True
            ).astype(jnp.float32),
            lax.psum_scatter(
                triple_add_slope.astype(jnp.bfloat16), "shard", scatter_dimension=0, tiled=True
            ).astype(jnp.float32),
            lax.psum_scatter(
                merger_slope.astype(jnp.bfloat16), "shard", scatter_dimension=0, tiled=True
            ).astype(jnp.float32),
            lax.psum_scatter(
                bias_slope.astype(jnp.bfloat16), "shard", scatter_dimension=0, tiled=True
            ).astype(jnp.float32),
            lax.psum_scatter(
                expander_slope.astype(jnp.bfloat16), "shard", scatter_dimension=0, tiled=True
            ).astype(jnp.float32),
            lax.psum_scatter(
                expander_add_slope.astype(jnp.bfloat16), "shard", scatter_dimension=0, tiled=True
            ).astype(jnp.float32),
            lax.psum_scatter(
                shrinker_slope.astype(jnp.bfloat16), "shard", scatter_dimension=0, tiled=True
            ).astype(jnp.float32),
            lax.psum_scatter(
                bias_slope.astype(jnp.bfloat16), "shard", scatter_dimension=0, tiled=True
            ).astype(jnp.float32),
        )
        owned = (
            lax.psum(owned[0].astype(jnp.bfloat16), "rep").astype(jnp.float32),
            lax.psum(owned[1].astype(jnp.bfloat16), "rep").astype(jnp.float32),
            lax.psum(owned[2].astype(jnp.bfloat16), "rep").astype(jnp.float32),
            lax.psum(owned[3].astype(jnp.bfloat16), "rep").astype(jnp.float32),
            lax.psum(owned[4].astype(jnp.bfloat16), "rep").astype(jnp.float32),
            lax.psum(owned[5].astype(jnp.bfloat16), "rep").astype(jnp.float32),
            lax.psum(owned[6].astype(jnp.bfloat16), "rep").astype(jnp.float32),
            lax.psum(owned[7].astype(jnp.bfloat16), "rep").astype(jnp.float32),
            lax.psum(owned[8].astype(jnp.bfloat16), "rep").astype(jnp.float32),
            lax.psum(owned[9].astype(jnp.bfloat16), "rep").astype(jnp.float32),
        )
        collected[layer] = owned
    stacked = tuple(
        (jnp.stack([collected[layer][index] for layer in range(LAYERS)]) for index in range(10))
    )
    return (
        hidden_out,
        slope,
        stacked[0],
        stacked[1],
        stacked[2],
        stacked[3],
        stacked[4],
        stacked[5],
        stacked[6],
        stacked[7],
        stacked[8],
        stacked[9],
        rms_stats,
    )


def solution(mesh):
    return jax.shard_map(
        body,
        mesh=mesh,
        in_specs=(
            P(("rep", "shard"), None),
            P("rep"),
            P(None, "shard"),
            P(None, "shard"),
            P(None, "shard", None),
            P(None, "shard"),
            P(None, "shard", None),
            P(None, "shard"),
            P(None, "shard", None),
            P(None, "shard"),
            P(None, "shard", None),
            P(None, "shard"),
            P(("rep", "shard"), None),
        ),
        out_specs=(
            P(("rep", "shard"), None),
            P(("rep", "shard"), None),
            P(None, "shard"),
            P(None, "shard"),
            P(None, "shard", None),
            P(None, "shard"),
            P(None, "shard", None),
            P(None, "shard"),
            P(None, "shard", None),
            P(None, "shard"),
            P(None, "shard", None),
            P(None, "shard"),
            P("rep", None),
        ),
        check_vma=False,
    )
```

profile of v0, /device:TPU:0, one launch (start us, length us, event | category | flops | bytes accessed | tf_op | source)
XLA Modules:
  0.0 1728.8 jit_solution(10861042924278429022)
XLA Ops:
  7.3 3.8 fusion.165
  11.2 5.1 all-gather
  16.2 5.3 all-gather.1
  21.6 5.2 all-gather.3
  27.3 49.5 %all-gather.41.cloned.1.call-done = bf16[1,1024,3072]{2,1,0:T(8,128)(2,1)} async-done(((bf16[1,256,3072]{2,1,0:T(8,128)(2,1)}), bf16[1,1024,3072]{2,1,0:T(8,128)(2,1)}) %all-gather.41.cloned.1.call-update) | async-done | bytes 6291472 | tf_op jit(solution)/shard_map/all_gather | solution.py:78
  76.8 3.9 fusion.30
  85.3 4.7 fusion.163
  90.1 4.7 fusion.164
  97.6 5.4 all-gather.5
  103.6 5.2 all-gather.7
  109.4 5.1 all-gather.9
  115.0 5.1 all-gather.10
  120.1 5.1 all-gather.11
  125.2 5.4 all-gather.13
  137.8 3.9 fusion.103
  141.8 19.0 %all-gather.43.cloned.1.call-done = bf16[1,1024,1024]{2,1,0:T(8,128)(2,1)} async-done(((bf16[1,256,1024]{2,1,0:T(8,128)(2,1)}), bf16[1,1024,1024]{2,1,0:T(8,128)(2,1)}) %all-gather.43.cloned.1.call-update) | async-done | bytes 2097168 | tf_op jit(solution)/shard_map/all_gather | solution.py:80
  163.7 80.5 %all-gather.45.cloned.1.call-done = bf16[1,1024,4096]{2,1,0:T(8,128)(2,1)} async-done(((bf16[1,256,4096]{2,1,0:T(8,128)(2,1)}), bf16[1,1024,4096]{2,1,0:T(8,128)(2,1)}) %all-gather.45.cloned.1.call-update) | async-done | bytes 8388624 | tf_op jit(solution)/shard_map/all_gather | solution.py:82
  244.3 4.8 fusion.24
  249.0 79.7 %all-gather.47.cloned.1.call-done = bf16[1,4096,1024]{2,1,0:T(8,128)(2,1)} async-done(((bf16[1,1024,1024]{2,1,0:T(8,128)(2,1)}), bf16[1,4096,1024]{2,1,0:T(8,128)(2,1)}) %all-gather.47.cloned.1.call-update) | async-done | bytes 8388624 | tf_op jit(solution)/shard_map/all_gather | solution.py:84
  328.7 5.8 fusion.161
  334.9 60.8 %all-gather.49.cloned.1.call-done = bf16[1,1024,3072]{2,1,0:T(8,128)(2,1)} async-done(((bf16[1,256,3072]{2,1,0:T(8,128)(2,1)}), bf16[1,1024,3072]{2,1,0:T(8,128)(2,1)}) %all-gather.49.cloned.1.call-update) | async-done | bytes 6291472 | tf_op jit(solution)/shard_map/all_gather | solution.py:78
  395.7 3.8 fusion.33
  407.8 20.9 %all-gather.51.cloned.1.call-done = bf16[1,1024,1024]{2,1,0:T(8,128)(2,1)} async-done(((bf16[1,256,1024]{2,1,0:T(8,128)(2,1)}), bf16[1,1024,1024]{2,1,0:T(8,128)(2,1)}) %all-gather.51.cloned.1.call-update) | async-done | bytes 2097168 | tf_op jit(solution)/shard_map/all_gather | solution.py:80
  431.4 20.8 %all-gather.37.cloned.1.call-done = bf16[512,1024]{1,0:T(8,128)(2,1)} async-done(((bf16[128,1024]{1,0:T(8,128)(2,1)}), bf16[512,1024]{1,0:T(8,128)(2,1)}) %all-gather.37.cloned.1.call-update) | async-done | bytes 1048592 | tf_op jit(solution)/shard_map/all_gather | solution.py:116
  453.7 21.9 %all-gather.39.cloned.1.call-done = bf16[512,1024]{0,1:T(8,128)(2,1)} async-done(((bf16[128,1024]{0,1:T(8,128)(2,1)}), bf16[512,1024]{0,1:T(8,128)(2,1)}) %all-gather.39.cloned.1.call-update) | async-done | bytes 1048592 | tf_op jit(solution)/shard_map/all_gather | solution.py:115
  486.7 5.5 all-gather.17
  492.3 5.3 all-gather.19
  498.2 5.1 all-gather.15
  504.5 54.9 %all-gather.53.cloned.1.call-done = bf16[1,1024,4096]{2,1,0:T(8,128)(2,1)} async-done(((bf16[1,256,4096]{2,1,0:T(8,128)(2,1)}), bf16[1,1024,4096]{2,1,0:T(8,128)(2,1)}) %all-gather.53.cloned.1.call-update) | async-done | bytes 8388624 | tf_op jit(solution)/shard_map/all_gather | solution.py:82
  559.4 6.0 fusion.27
  565.4 78.5 %all-gather.55.cloned.1.call-done = bf16[1,4096,1024]{2,1,0:T(8,128)(2,1)} async-done(((bf16[1,1024,1024]{2,1,0:T(8,128)(2,1)}), bf16[1,4096,1024]{2,1,0:T(8,128)(2,1)}) %all-gather.55.cloned.1.call-update) | async-done | bytes 8388624 | tf_op jit(solution)/shard_map/all_gather | solution.py:84
  643.9 8.7 fusion.175
  657.1 6.6 fusion.99
  669.9 22.4 %reduce-scatter.39.cloned.1.call-done = bf16[128,1024]{1,0:T(8,128)(2,1)} async-done(((bf16[512,1024]{1,0:T(8,128)(2,1)}), bf16[128,1024]{1,0:T(8,128)(2,1)}) %reduce-scatter.39.cloned.1.call-update) | async-done | bytes 262160
  693.5 5.1 fusion.16
  698.7 7.1 multiply_reduce_fusion.7
  709.8 3.9 multiply_reduce_fusion
  719.1 4.1 fusion.81
  731.1 5.6 convolution_convert_fusion.4
  736.8 7.0 convolution_convert_fusion.2
  743.8 7.3 convolution_convert_fusion
  755.3 9.7 reduce-scatter.43.cloned.1.call-done
  767.0 4.7 convolution_convert_fusion.5
  773.3 7.0 fusion.176
  781.3 5.9 convolution_convert_fusion.3
  787.2 5.7 convolution_convert_fusion.1
  793.2 3.6 reduce-scatter.27.cloned.1.call-done
  796.7 31.7 %reduce-scatter.25.cloned.1.call-done = bf16[256,1024]{1,0:T(8,128)(2,1)} async-done(((bf16[1024,1024]{1,0:T(8,128)(2,1)}), bf16[256,1024]{1,0:T(8,128)(2,1)}) %reduce-scatter.25.cloned.1.call-update) | async-done | bytes 524304 | tf_op jit(solution)/shard_map/reduce_scatter | solution.py:263
  828.4 66.6 %reduce-scatter.23.cloned.1.call-done = bf16[256,3072]{1,0:T(8,128)(2,1)} async-done(((bf16[1024,3072]{1,0:T(8,128)(2,1)}), bf16[256,3072]{1,0:T(8,128)(2,1)}) %reduce-scatter.23.cloned.1.call-update) | async-done | bytes 1572880 | tf_op jit(solution)/shard_map/reduce_scatter | solution.py:257
  894.9 83.0 %reduce-scatter.31.cloned.1.call-done = bf16[256,4096]{1,0:T(8,128)(2,1)} async-done(((bf16[1024,4096]{1,0:T(8,128)(2,1)}), bf16[256,4096]{1,0:T(8,128)(2,1)}) %reduce-scatter.31.cloned.1.call-update) | async-done | bytes 2097168 | tf_op jit(solution)/shard_map/reduce_scatter | solution.py:269
  977.9 82.6 %reduce-scatter.35.cloned.1.call-done = bf16[1024,1024]{1,0:T(8,128)(2,1)} async-done(((bf16[4096,1024]{1,0:T(8,128)(2,1)}), bf16[1024,1024]{1,0:T(8,128)(2,1)}) %reduce-scatter.35.cloned.1.call-update) | async-done | bytes 2097168 | tf_op jit(solution)/shard_map/reduce_scatter | solution.py:275
  1060.5 66.0 %reduce-scatter.21.cloned.1.call-done = bf16[256,3072]{1,0:T(8,128)(2,1)} async-done(((bf16[1024,3072]{1,0:T(8,128)(2,1)}), bf16[256,3072]{1,0:T(8,128)(2,1)}) %reduce-scatter.21.cloned.1.call-update) | async-done | bytes 1572880 | tf_op jit(solution)/shard_map/reduce_scatter | solution.py:257
  1126.5 83.1 %reduce-scatter.29.cloned.1.call-done = bf16[256,4096]{1,0:T(8,128)(2,1)} async-done(((bf16[1024,4096]{1,0:T(8,128)(2,1)}), bf16[256,4096]{1,0:T(8,128)(2,1)}) %reduce-scatter.29.cloned.1.call-update) | async-done | bytes 2097168 | tf_op jit(solution)/shard_map/reduce_scatter | solution.py:269
  1209.6 82.4 %reduce-scatter.33.cloned.1.call-done = bf16[1024,1024]{1,0:T(8,128)(2,1)} async-done(((bf16[4096,1024]{1,0:T(8,128)(2,1)}), bf16[1024,1024]{1,0:T(8,128)(2,1)}) %reduce-scatter.33.cloned.1.call-update) | async-done | bytes 2097168 | tf_op jit(solution)/shard_map/reduce_scatter | solution.py:275
  1295.2 5.1 fusion.20
  1300.4 6.4 fusion.156
  1307.5 4.0 stack.192
  1312.8 6.7 psum.157
  1320.2 15.3 all-reduce.12
  1336.2 182.9 %all-reduce.10 = (bf16[1,256]{1,0:T(2,128)(2,1)S(1)}, bf16[1,256]{1,0:T(2,128)(2,1)S(1)}, bf16[1,256]{1,0:T(2,128)(2,1)S(1)}, bf16[1,256]{1,0:T(2,128)(2,1)S(1)}...) all-reduce(bf16[1,256]{1,0:T(2,128)(2,1)S(1)} %stack.151, ...), channel_id=1, replica_groups=mesh['rep'=32,'shard'=4] {'rep'}, use_global_device_ids=true, to_apply=%region_23.24 | all-reduce | flops 5120 | bytes 20480 | tf_op jit(solution)/shard_map/psum | solution.py:283
  1522.5 183.0 %all-reduce.15.cloned.1.call-done = (bf16[1,256,3072]{2,1,0:T(8,128)(2,1)}, bf16[1,256,3072]{2,1,0:T(8,128)(2,1)}, bf16[1,256,1024]{2,1,0:T(8,128)(2,1)}, bf16[1...) async-done(((bf16[1,256,3072]{2,1,0:T(8,128)(2,1)}, ...) | async-done | bytes 12582928 | tf_op jit(solution)/shard_map/psum | solution.py:285
  1705.5 6.3 maximum_convert_fusion.1
  1711.8 3.9 maximum_convert_fusion
  1718.4 3.1 maximum_convert_fusion.2
  (365 shorter events, 93.9 us)
Async XLA Ops:
  7.2 9.0 copy-start.74
  7.2 14.4 copy-start.65
  7.2 19.6 %copy-start.5 = (bf16[128,1024]{1,0:T(8,128)(2,1)S(1)}, bf16[128,1024]{1,0:T(8,128)(2,1)}, u32[]{:S(2)}) copy-start(bf16[128,1024]{1,0:T(8,128)(2,1)} %param.13) | copy-start | bytes 786436
  7.2 69.6 %all-gather.41.cloned.1.call-start = ((), (), s32[]{:S(2)}) async-start(), calls=%async_computation.24 | async-start | bytes 7864320 | tf_op jit(solution)/shard_map/all_gather | solution.py:78
  11.1 119.7 %all-gather.35.cloned.1.call-start = ((), (), s32[]{:S(2)}) async-start(), calls=%async_computation.13 | async-start | bytes 1310720 | tf_op jit(solution)/shard_map/all_gather | solution.py:115
  27.2 53.5 %copy-start.81 = (f32[128]{0:T(128)}, f32[128]{0:T(128)S(1)}, u32[]{:S(2)}) copy-start(f32[128]{0:T(128)S(1)} %fusion.119) | copy-start | bytes 1540
  27.2 217.1 %copy-start.55 = (f32[128]{0:T(128)}, f32[128]{0:T(128)S(1)}, u32[]{:S(2)}) copy-start(f32[128]{0:T(128)S(1)} %fusion.131) | copy-start | bytes 1540
  81.4 49.5 %copy-start.43 = (f32[128,16,16]{0,2,1:T(8,128)}, f32[128,16,16]{0,2,1:T(8,128)S(1)}, u32[]{:S(2)}) copy-start(f32[128,16,16]{0,2,1:T(8,128)S(1)} %get-tuple-element.88) | copy-start | bytes 393220
  81.4 49.5 %copy-start.45 = (f32[128,16,16]{0,2,1:T(8,128)}, f32[128,16,16]{0,2,1:T(8,128)S(1)}, u32[]{:S(2)}) copy-start(f32[128,16,16]{0,2,1:T(8,128)S(1)} %get-tuple-element.89) | copy-start | bytes 393220
  82.2 54.2 %all-gather.33.cloned.1.call-start = ((), (), s32[]{:S(2)}) async-start(), calls=%async_computation.12 | async-start | bytes 1310720 | tf_op jit(solution)/shard_map/all_gather | solution.py:116
  83.0 77.9 %all-gather.43.cloned.1.call-start = ((), (), s32[]{:S(2)}) async-start(), calls=%async_computation.25 | async-start | bytes 2621440 | tf_op jit(solution)/shard_map/all_gather | solution.py:80
  85.3 159.0 %all-gather.45.cloned.1.call-start = ((), (), s32[]{:S(2)}) async-start(), calls=%async_computation.26 | async-start | bytes 10485760 | tf_op jit(solution)/shard_map/all_gather | solution.py:82
  90.1 238.6 %all-gather.47.cloned.1.call-start = ((), (), s32[]{:S(2)}) async-start(), calls=%async_computation.27 | async-start | bytes 10485760 | tf_op jit(solution)/shard_map/all_gather | solution.py:84
  94.8 8.2 copy-start.63
  94.8 14.0 copy-start.76
  94.8 300.8 %all-gather.49.cloned.1.call-start = ((), (), s32[]{:S(2)}) async-start(), calls=%async_computation.28 | async-start | bytes 7864320 | tf_op jit(solution)/shard_map/all_gather | solution.py:78
  95.6 333.1 %all-gather.51.cloned.1.call-start = ((), (), s32[]{:S(2)}) async-start(), calls=%async_computation.29 | async-start | bytes 2621440 | tf_op jit(solution)/shard_map/all_gather | solution.py:80
  96.3 355.9 %all-gather.37.cloned.1.call-start = ((), (), s32[]{:S(2)}) async-start(), calls=%async_computation.14 | async-start | bytes 1310720 | tf_op jit(solution)/shard_map/all_gather | solution.py:116
  141.8 107.2 %copy-start.49 = (bf16[16,64,128]{2,1,0:T(8,128)(2,1)}, bf16[16,64,128]{2,1,0:T(8,128)(2,1)S(1)}, u32[]{:S(2)}) copy-start(bf16[16,64,128]{2,1,0:T(8,128)(2,1)S(1)} %fusion.103) | copy-start | bytes 786436
  244.2 84.5 %copy-start.71 = (f32[1,1024]{1,0:T(1,128)S(1)}, f32[1,1024]{1,0:T(1,128)}, u32[]{:S(2)}) copy-start(f32[1,1024]{1,0:T(1,128)} %convert_element_type.365) | copy-start | bytes 12292
  249.0 85.5 %copy-start.6 = (f32[128,4096]{1,0:T(8,128)}, f32[128,4096]{1,0:T(8,128)S(1)}, u32[]{:S(2)}) copy-start(f32[128,4096]{1,0:T(8,128)S(1)} %fusion.24) | copy-start | bytes 6291460
  334.5 65.0 %copy-start.67 = (f32[128]{0:T(128)}, f32[128]{0:T(128)S(1)}, u32[]{:S(2)}) copy-start(f32[128]{0:T(128)S(1)} %broadcast_multiply_fusion) | copy-start | bytes 1540
  334.7 64.8 %copy-start.85 = (f32[128]{0:T(128)}, f32[128]{0:T(128)S(1)}, u32[]{:S(2)}) copy-start(f32[128]{0:T(128)S(1)} %multiply_reduce_fusion.9) | copy-start | bytes 1540
  334.7 64.8 %copy-start.69 = (f32[128]{0:T(128)}, f32[128]{0:T(128)S(1)}, u32[]{:S(2)}) copy-start(f32[128]{0:T(128)S(1)} %fusion.132) | copy-start | bytes 1540
  400.3 75.3 %all-gather.39.cloned.1.call-start = ((), (), s32[]{:S(2)}) async-start(), calls=%async_computation.15 | async-start | bytes 1310720 | tf_op jit(solution)/shard_map/all_gather | solution.py:115
  405.4 154.0 %all-gather.53.cloned.1.call-start = ((), (), s32[]{:S(2)}) async-start(), calls=%async_computation.30 | async-start | bytes 10485760 | tf_op jit(solution)/shard_map/all_gather | solution.py:82
  405.4 23.3 %copy-start.10 = (bf16[128,1024]{1,0:T(8,128)(2,1)S(1)}, bf16[128,1024]{1,0:T(8,128)(2,1)}, u32[]{:S(2)}) copy-start(bf16[128,1024]{1,0:T(8,128)(2,1)} %param.25) | copy-start | bytes 786436
  406.1 237.7 %all-gather.55.cloned.1.call-start = ((), (), s32[]{:S(2)}) async-start(), calls=%async_computation.31 | async-start | bytes 10485760 | tf_op jit(solution)/shard_map/all_gather | solution.py:84
  406.7 261.8 %reduce-scatter.37.cloned.1.call-start = ((), (), s32[]{:S(2)}) async-start(), calls=%async_computation.32 | async-start | bytes 1310720
  407.8 45.9 %copy-start.60 = (f32[128]{0:T(128)}, f32[128]{0:T(128)S(1)}, u32[]{:S(2)}) copy-start(f32[128]{0:T(128)S(1)} %get-tuple-element.60) | copy-start | bytes 1540
  431.3 48.5 %copy-start.27 = (bf16[128,1024]{0,1:T(8,128)(2,1)}, bf16[128,1024]{0,1:T(8,128)(2,1)S(1)}, u32[]{:S(2)}) copy-start(bf16[128,1024]{0,1:T(8,128)(2,1)S(1)} %copy.58) | copy-start | bytes 786436
  431.4 46.5 %copy-start.23 = (f32[128,16,32]{0,2,1:T(8,128)}, f32[128,16,32]{0,2,1:T(8,128)S(1)}, u32[]{:S(2)}) copy-start(f32[128,16,32]{0,2,1:T(8,128)S(1)} %slice.229) | copy-start | bytes 786436
  453.7 26.1 %copy-start.17 = (bf16[512,1024]{0,1:T(8,128)(2,1)}, bf16[512,1024]{0,1:T(8,128)(2,1)S(1)}, u32[]{:S(2)}) copy-start(bf16[512,1024]{0,1:T(8,128)(2,1)S(1)} %copy.55) | copy-start | bytes 3145732
  484.3 13.8 copy-start.77
  486.6 205.7 %reduce-scatter.39.cloned.1.call-start = ((), (), s32[]{:S(2)}) async-start(), calls=%async_computation.33 | async-start | bytes 1310720
  559.4 84.5 %copy-start.61 = (f32[128]{0:T(128)S(1)}, f32[128]{0:T(128)}, u32[]{:S(2)}) copy-start(f32[128]{0:T(128)} %copy-done.60) | copy-start | bytes 1540
  643.9 8.8 copy-start.3
  643.9 8.8 copy-start.28
  656.9 97.2 %reduce-scatter.41.cloned.1.call-start = ((), (), s32[]{:S(2)}) async-start(), calls=%async_computation.34 | async-start | bytes 1310720
  657.1 6.6 copy-start.19
  657.1 8.2 copy-start.4
  667.0 38.8 %copy-start.50 = (bf16[16,64,128]{2,1,0:T(8,128)(2,1)}, bf16[16,64,128]{2,1,0:T(8,128)(2,1)S(1)}, u32[]{:S(2)}) copy-start(bf16[16,64,128]{2,1,0:T(8,128)(2,1)S(1)} %fusion.102) | copy-start | bytes 786436
  669.9 28.7 %copy-start.31 = (bf16[128,16,64]{0,2,1:T(8,128)(2,1)}, bf16[128,16,64]{0,2,1:T(8,128)(2,1)S(1)}, u32[]{:S(2)}) copy-start(bf16[128,16,64]{0,2,1:T(8,128)(2,1)S(1)} %fusion.125) | copy-start | bytes 786436
  669.9 28.7 %copy-start.33 = (bf16[128,16,64]{0,2,1:T(8,128)(2,1)}, bf16[128,16,64]{0,2,1:T(8,128)(2,1)S(1)}, u32[]{:S(2)}) copy-start(bf16[128,16,64]{0,2,1:T(8,128)(2,1)S(1)} %pad_maximum_fusion.4) | copy-start | bytes 786436
  698.7 7.2 copy-start.86
  698.7 7.2 copy-start.9
  698.7 7.2 copy-start.52
  698.7 7.2 copy-start.62
  719.0 46.0 %reduce-scatter.43.cloned.1.call-start = ((), (), s32[]{:S(2)}) async-start(), calls=%async_computation.35 | async-start | bytes 1310720
  725.5 71.2 %reduce-scatter.27.cloned.1.call-start = ((), (), s32[]{:S(2)}) async-start(), calls=%async_computation.19 | async-start | bytes 2621440 | tf_op jit(solution)/shard_map/reduce_scatter | solution.py:263
  728.0 100.4 %reduce-scatter.25.cloned.1.call-start = ((), (), s32[]{:S(2)}) async-start(), calls=%async_computation.18 | async-start | bytes 2621440 | tf_op jit(solution)/shard_map/reduce_scatter | solution.py:263
  731.1 163.9 %reduce-scatter.23.cloned.1.call-start = ((), (), s32[]{:S(2)}) async-start(), calls=%async_computation.17 | async-start | bytes 7864320 | tf_op jit(solution)/shard_map/reduce_scatter | solution.py:257
  736.7 241.2 %reduce-scatter.31.cloned.1.call-start = ((), (), s32[]{:S(2)}) async-start(), calls=%async_computation.21 | async-start | bytes 10485760 | tf_op jit(solution)/shard_map/reduce_scatter | solution.py:269
  743.8 316.7 %reduce-scatter.35.cloned.1.call-start = ((), (), s32[]{:S(2)}) async-start(), calls=%async_computation.23 | async-start | bytes 10485760 | tf_op jit(solution)/shard_map/reduce_scatter | solution.py:275
  751.1 375.3 %reduce-scatter.21.cloned.1.call-start = ((), (), s32[]{:S(2)}) async-start(), calls=%async_computation.16 | async-start | bytes 7864320 | tf_op jit(solution)/shard_map/reduce_scatter | solution.py:257
  754.0 12.1 copy-start.36
  754.0 12.2 slice-start
  754.1 13.0 copy-start.56
  771.7 437.9 %reduce-scatter.29.cloned.1.call-start = ((), (), s32[]{:S(2)}) async-start(), calls=%async_computation.20 | async-start | bytes 10485760 | tf_op jit(solution)/shard_map/reduce_scatter | solution.py:269
  787.2 504.8 %reduce-scatter.33.cloned.1.call-start = ((), (), s32[]{:S(2)}) async-start(), calls=%async_computation.22 | async-start | bytes 10485760 | tf_op jit(solution)/shard_map/reduce_scatter | solution.py:275
  792.9 912.5 %all-reduce.15.cloned.1.call-start = ((), (), s32[]{:S(2)}) async-start(), calls=%async_computation.36 | async-start | bytes 25165824 | tf_op jit(solution)/shard_map/psum | solution.py:285
  1300.4 19.4 %copy-start.82 = (f32[128]{0:T(128)S(1)}, f32[128]{0:T(128)}, u32[]{:S(2)}) copy-start(f32[128]{0:T(128)} %copy-done.81) | copy-start | bytes 1540
  1306.8 214.6 %copy-start.12 = (f32[128,1024]{1,0:T(8,128)S(1)}, f32[128,1024]{1,0:T(8,128)}, u32[]{:S(2)}) copy-start(f32[128,1024]{1,0:T(8,128)} %copy-done.11) | copy-start | bytes 1572868
  1519.1 202.4 %copy-start.66 = (f32[2,256]{1,0:T(2,128)}, f32[2,256]{1,0:T(2,128)S(1)}, u32[]{:S(2)}) copy-start(f32[2,256]{1,0:T(2,128)S(1)} %maximum_convert_fusion.8) | copy-start | bytes 6148
  (51 other events, 161.4 us)
Sparse Core Ops, SparseCore 0:
  11.2 65.5 all-gather.40
  82.3 22.0 all-gather.34
  106.7 22.5 all-gather.32
  130.8 29.9 all-gather.42
  162.9 81.2 all-gather.44
  246.3 82.3 all-gather.46
  330.4 65.2 all-gather.48
  397.9 30.7 all-gather.50
  430.4 21.7 all-gather.36
  454.3 21.2 all-gather.38
  477.3 82.0 all-gather.52
  561.5 82.3 all-gather.54
  646.3 22.2 reduce-scatter.36
  670.9 21.3 reduce-scatter.38
  719.2 21.4 reduce-scatter.40
  743.6 21.3 reduce-scatter.42
  767.3 29.4 reduce-scatter.26
  799.1 29.2 reduce-scatter.24
  831.4 63.5 reduce-scatter.22
  897.8 80.0 reduce-scatter.30
  980.4 80.0 reduce-scatter.34
  1062.9 63.4 reduce-scatter.20
  1129.5 80.0 reduce-scatter.28
  1211.9 80.0 reduce-scatter.32
  1295.1 410.2 all-reduce.14
where the time goes:
time: 1730 us
  waiting for transfers between devices  1200 us (69%)
  blocking collectives  267 us (15%)
  matrix products  147 us (8%)
  local copies, waits for them, and re-layouts  55.7 us (3%)
  other arithmetic  33.3 us (2%)
  between operations  18.3 us (1%)
    psum x1, waiting for transfers between devices, body(): lax.psum(owned[2].astype(jnp.bfloat16), 'rep').astype(jnp.float32)  183 us
    psum x1, blocking collectives, body(): lax.psum(owned[0].astype(jnp.bfloat16), 'rep').astype(jnp.float32)  183 us
    reduce_scatter x2, waiting for transfers between devices, body(): lax.psum_scatter(expander_slope.astype(jnp.bfloat16), 'shard', scatter_di...  166 us
    reduce_scatter x2, waiting for transfers between devices, body(): lax.psum_scatter(shrinker_slope.astype(jnp.bfloat16), 'shard', scatter_di...  165 us
    all_gather x2, waiting for transfers between devices, body(): lax.all_gather(shrinker[layer], 'shard', axis=0, tiled=True)  158 us
    all_gather x2, waiting for transfers between devices, body(): lax.all_gather(expander[layer], 'shard', axis=0, tiled=True)  135 us
    reduce_scatter x2, waiting for transfers between devices, body(): lax.psum_scatter(triple_slope.astype(jnp.bfloat16), 'shard', scatter_dime...  133 us
    all_gather x2, waiting for transfers between devices, body(): lax.all_gather(triple[layer], 'shard', axis=0, tiled=True)  110 us
  transfers between devices with their start and end apart: 25, of which 22 were waited for; matrix products, arithmetic and copies ran while one was open for 10% of the time, Pallas kernels for 0%

commit v1 on v0

v1 whole, which is shorter than its diff:
```python
import functools
import math

import jax
import jax.numpy as jnp
from jax import lax
from jax.experimental import pallas as pl
from jax.experimental.pallas import tpu as pltpu
from jax.sharding import PartitionSpec as P

HD = 64
ROT = 32
LAYERS = 2
EPS_NORM = 1e-05
AXES = ("rep", "shard")
BF = jnp.bfloat16
F32 = jnp.float32
MINE = 4
W = 1024
WIDE = 1792
CHUNK = 1536

VM = pl.BlockSpec(memory_space=pltpu.VMEM)
ANY = pl.BlockSpec(memory_space=pl.ANY)
SM = pl.BlockSpec(memory_space=pltpu.SMEM)


def place_of(index):
    rep, shard = divmod(index, 4)
    x, rest = divmod(rep, 8)
    z_hi, y = divmod(rest, 4)
    z_lo, core = divmod(shard, 2)
    return x, y, z_hi * 2 + z_lo, core


def index_of(x, y, z, core):
    return ((x * 2 + z // 2) * 4 + y) * 4 + (z % 2) * 2 + core


def move(value, dx=0, dy=0, flip_z=0, flip_core=0):
    pairs = []
    for index in range(128):
        x, y, z, core = place_of(index)
        target = index_of((x + dx) % 4, (y + dy) % 4, z ^ flip_z, core ^ flip_core)
        pairs.append((index, target))
    return lax.ppermute(value, AXES, pairs)


def step(value, axis, by):
    return move(value, dx=by) if axis == 0 else move(value, dy=by)


def after(value, *others):
    return lax.optimization_barrier((value,) + others)[0]


def pick(value, index, axis=0):
    return lax.dynamic_index_in_dim(value, index, axis, keepdims=False)


def shape(*dims, dtype=BF):
    return jax.ShapeDtypeStruct(dims, dtype)


def call(body, args, specs, outs, out_specs=None, scratch=(), flops=0, aliases=None):
    moved = sum(math.prod(o.shape) * o.dtype.itemsize for o in outs)
    moved += sum(math.prod(a.shape) * a.dtype.itemsize for a, s in zip(args, specs) if s is VM)
    return pl.pallas_call(
        body,
        out_shape=outs,
        in_specs=specs,
        out_specs=out_specs or [VM] * len(outs),
        scratch_shapes=scratch,
        input_output_aliases=aliases or {},
        compiler_params=pltpu.CompilerParams(vmem_limit_bytes=56 * 2**20),
        cost_estimate=pl.CostEstimate(flops=flops, bytes_accessed=moved, transcendentals=0),
    )(*args)


def dot(left, right):
    return jnp.dot(left, right, preferred_element_type=F32)


def dot_t(left, right):
    return lax.dot_general(left, right, (((1,), (1,)), ((), ())), preferred_element_type=F32)


def t_dot(left, right):
    return lax.dot_general(left, right, (((0,), (0,)), ((), ())), preferred_element_type=F32)


def copies(pairs, sems):
    started = []
    for at, (source, target) in enumerate(pairs):
        copy = pltpu.make_async_copy(source, target, sems.at[at])
        copy.start()
        started.append(copy)
    return started


def finish(started):
    for copy in started:
        copy.wait()


def lanes(start, size):
    return pl.ds(pl.multiple_of(start, 128), size)


def rows_at(start, size):
    return pl.ds(pl.multiple_of(start, 16), size)


def cut_triple(place, triple, out1, out2a, out2b, out3a, out3b, slab, sems):
    shard = place[2]
    finish(copies([(triple.at[0], slab)], sems))
    for k, refs in ((2, (out2a, out2b)), (3, (out3a, out3b)), (1, (out1,))):
        block = shard ^ k
        size = 256 // len(refs)
        for at, ref in enumerate(refs):
            for p in range(3):
                ref[:, pl.ds(p * 256, 256)] = slab[
                    pl.ds(at * size, size), lanes(p * W + block * 256, 256)
                ]


def cut_rest(
    place, triple, expander, e1, e2a, e2b, e3a, e3b, w1, w2, w3, slab, first, second, sems
):
    shard = place[2]
    pairs = [(expander.at[0], first), (expander.at[1], second), (triple.at[1], slab)]
    started = copies(pairs, sems)
    started[0].wait()
    for k, refs in ((2, (e2a, e2b)), (3, (e3a, e3b)), (1, (e1,))):
        size = 256 // len(refs)
        for at, ref in enumerate(refs):
            ref[...] = first[pl.ds(at * size, size), lanes((shard ^ k) * W, W)]
    finish(started[1:])
    for k, ref in ((2, w2), (3, w3), (1, w1)):
        block = shard ^ k
        ref[:, pl.ds(0, W)] = second[:, lanes(block * W, W)]
        for p in range(3):
            ref[:, pl.ds(W + p * 256, 256)] = slab[:, lanes(p * W + block * 256, 256)]


def own_triple(shard, layer, triple, wide):
    return [
        (
            triple.at[layer, :, lanes(p * W + shard * 256, 256)],
            wide.at[rows_at(shard * 256, 256), pl.ds(W + p * 256, 256)],
        )
        for p in range(3)
    ]


def own_expander(shard, layer, expander, wide):
    return [
        (expander.at[layer, :, lanes(shard * W, W)], wide.at[rows_at(shard * 256, 256), pl.ds(0, W)])
    ]


def first_triple(shard, pieces, wide):
    pairs = []
    one, two_a, two_b, three_a, three_b = pieces
    for k, refs in ((1, (one,)), (2, (two_a, two_b)), (3, (three_a, three_b))):
        size = 256 // len(refs)
        for at, ref in enumerate(refs):
            target = wide.at[rows_at((shard ^ k) * 256 + at * size, size), pl.ds(W, 768)]
            pairs.append((ref, target))
    return pairs


def first_expander(shard, pieces, wide):
    pairs = []
    one, two_a, two_b, three_a, three_b = pieces
    for k, refs in ((1, (one,)), (2, (two_a, two_b)), (3, (three_a, three_b))):
        size = 256 // len(refs)
        for at, ref in enumerate(refs):
            pairs.append((ref, wide.at[rows_at((shard ^ k) * 256 + at * size, size), pl.ds(0, W)]))
    return pairs


def second_wide(shard, pieces, wide):
    return [
        (ref, wide.at[rows_at((shard ^ k) * 256, 256), :]) for k, ref in zip((1, 2, 3), pieces)
    ]


def spots(shard):
    row = lax.broadcasted_iota(jnp.int32, (512, 1), 0)
    col = lax.broadcasted_iota(jnp.int32, (1, 512), 1)

    def at(i):
        return (((i >> 7) ^ shard) << 7) | (i & 127)

    return at(row), at(col)


def rotate(values, turn, back=False):
    ahead = pltpu.roll(values, 256 - 16, 1) * turn[1]
    behind = pltpu.roll(values, 16, 1) * turn[2]
    if back:
        return values * turn[0] - ahead - behind
    return values * turn[0] + ahead + behind


def normalize(state):
    mean = jnp.mean(state, axis=-1, keepdims=True)
    centred = state - mean
    spread = jnp.mean(centred * centred, axis=-1, keepdims=True)
    factor = lax.rsqrt(spread + EPS_NORM)
    return centred * factor, factor


ROOT = math.sqrt(2.0 / math.pi)


def gelu_both(v):
    square = v * v
    t = jnp.tanh(ROOT * v * (1.0 + 0.044715 * square))
    half = 0.5 * (1.0 + t)
    slope = half + 0.5 * v * (1.0 - t * t) * (ROOT + (3.0 * 0.044715 * ROOT) * square)
    return v * half, slope


def heads_out(normed, wide, bias, turn, qkv):
    scale = HD ** (-0.5)
    for p in range(3):
        part = dot(normed[...], wide[:, pl.ds(W + p * 256, 256)]) + bias[:, pl.ds(p * 256, 256)]
        if p < 2:
            part = rotate(part, turn)
        if p == 0:
            part = part * scale
        qkv[:, pl.ds(p * 256, 256)] = part.astype(BF)


def probabilities(qkv, h, allowed):
    q = qkv[:, pl.ds(h * HD, HD)]
    k = qkv[:, pl.ds(256 + h * HD, HD)]
    scores = jnp.where(allowed, dot_t(q, k), -1000000000.0)
    powered = jnp.exp(scores - jnp.max(scores, axis=-1, keepdims=True))
    return powered * (1.0 / jnp.sum(powered, axis=-1, keepdims=True))


def attend(qkv, allowed, mixed):
    for h in range(MINE):
        low = probabilities(qkv, h, allowed).astype(BF)
        mixed[:, pl.ds(h * HD, HD)] = dot(low, qkv[:, pl.ds(512 + h * HD, HD)]).astype(BF)


def attend_back(qkv, allowed, mixed, slope_mixed, slopes, forward):
    for h in range(MINE):
        probs = probabilities(qkv, h, allowed)
        low = probs.astype(BF)
        q = qkv[:, pl.ds(h * HD, HD)]
        k = qkv[:, pl.ds(256 + h * HD, HD)]
        v = qkv[:, pl.ds(512 + h * HD, HD)]
        if forward:
            mixed[:, pl.ds(h * HD, HD)] = dot(low, v).astype(BF)
        out = slope_mixed[:, pl.ds(h * HD, HD)]
        slope_probs = dot_t(out, v)
        centre = jnp.sum(probs * slope_probs, axis=-1, keepdims=True)
        slope_scores = (probs * (slope_probs - centre)).astype(BF)
        slopes[:, pl.ds(h * HD, HD)] = dot(slope_scores, k)
        slopes[:, pl.ds(256 + h * HD, HD)] = t_dot(slope_scores, q)
        slopes[:, pl.ds(512 + h * HD, HD)] = t_dot(low, out)


def hand_out(left, right, send, keep):
    for n in range(4):
        cols = pl.ds(n * 256, 256)
        part = dot(left[...], right[:, cols])
        spread_out(part, cols, send, keep)


def spread_out(part, cols, send, keep):
    keep[pl.ds(0, 128), cols] = part[0:128]
    send[pl.ds(0, 128), cols] = part[128:256].astype(BF)
    keep[pl.ds(128, 128), cols] = part[256:384]
    send[pl.ds(128, 128), cols] = part[384:512].astype(BF)


def first_attention(
    place, x0, x1, x2, x3, vec, turn, triple, merger, t1, t2a, t2b, t3a, t3b,
    normed, qkv, mixed, send, keep, wide, merge, sems,
):
    shard, length = place[2], place[3]
    pairs = own_triple(shard, 0, triple, wide) + [(merger.at[0], merge)]
    started = copies(pairs + first_triple(shard, (t1, t2a, t2b, t3a, t3b), wide), sems)
    gain, shift = vec[pl.ds(0, 1), :], vec[pl.ds(2, 1), :]
    for k, ref in enumerate((x0, x1, x2, x3)):
        hat, _ = normalize(ref[...].astype(F32))
        normed[pl.ds(k * 128, 128), :] = (hat * gain + shift).astype(BF)
    finish(started)
    row, col = spots(shard)
    allowed = (col <= row) & (col < length)
    heads_out(normed, wide, vec[pl.ds(8, 1), pl.ds(0, 768)], turn, qkv)
    attend(qkv, allowed, mixed)
    hand_out(mixed, merge, send, keep)


def first_forward(
    place, normed, vec, expander, shrinker, e1, e2a, e2b, e3a, e3b,
    before, send, keep, wide, shrink, act, sems,
):
    shard = place[2]
    pairs = own_expander(shard, 0, expander, wide) + first_expander(shard, (e1, e2a, e2b, e3a, e3b), wide)
    started = copies(pairs + [(shrinker.at[0], shrink)], sems)
    finish(started)
    for n in range(4):
        cols = pl.ds(n * 256, 256)
        part = dot(normed[...], wide[:, cols]) + vec[pl.ds(10, 1), cols]
        before[:, cols] = part
        act[:, cols] = gelu_both(part)[0].astype(BF)
    hand_out(act, shrink, send, keep)


def slopes_out(ss, bias, wide, send, keep):
    bias[...] = jnp.broadcast_to(jnp.sum(ss[...].astype(F32), axis=0, keepdims=True), bias.shape)
    for n in range(4):
        part = dot_t(ss[...], wide[pl.ds(n * 256, 256), :])
        spread_out(part, pl.ds(n * 256, 256), send, keep)


def triple_slopes(slopes, turn, ss):
    scale = HD ** (-0.5)
    ss[:, pl.ds(W, 256)] = (rotate(slopes[:, pl.ds(0, 256)], turn, True) * scale).astype(BF)
    ss[:, pl.ds(W + 256, 256)] = rotate(slopes[:, pl.ds(256, 256)], turn, True).astype(BF)
    ss[:, pl.ds(W + 512, 256)] = slopes[:, pl.ds(512, 256)].astype(BF)


def last_layer(
    place, n0, n1, n2, n3, u0, u1, u2, u3, vec, turn, triple, merger, expander, shrinker, w1, w2, w3,
    normed, up, act, ss, mixed, asend, akeep, fsend, fkeep, send, keep, bias,
    wide, merge, shrink, qkv, slopes, out, before, sems,
):
    shard, length = place[2], place[3]
    pairs = own_triple(shard, 1, triple, wide) + own_expander(shard, 1, expander, wide)
    pairs += second_wide(shard, (w1, w2, w3), wide) + [(merger.at[1], merge), (shrinker.at[1], shrink)]
    started = copies(pairs, sems)
    row, col = spots(shard)
    for k, (n, u) in enumerate(((n0, u0), (n1, u1), (n2, u2), (n3, u3))):
        rows = pl.ds(k * 128, 128)
        normed[rows, :] = n[...]
        up[rows, :] = jnp.where(row[k * 128 : k * 128 + 128] < length, u[...].astype(F32), 0.0).astype(BF)
    finish(started)
    for n in range(4):
        cols = pl.ds(n * 256, 256)
        part = dot(normed[...], wide[:, cols]) + vec[pl.ds(11, 1), cols]
        value, slope = gelu_both(part)
        act[:, cols] = value.astype(BF)
        ss[:, cols] = (dot_t(up[...], shrink[cols, :]) * slope).astype(BF)
    hand_out(act, shrink, fsend, fkeep)
    allowed = (col <= row) & (col < length)
    heads_out(normed, wide, vec[pl.ds(9, 1), pl.ds(0, 768)], turn, qkv)
    out[...] = dot_t(up[...], merge[...]).astype(BF)
    attend_back(qkv, allowed, mixed, out, slopes, True)
    hand_out(mixed, merge, asend, akeep)
    triple_slopes(slopes, turn, ss)
    slopes_out(ss, bias, wide, send, keep)


def first_back(
    place, u0, u1, u2, u3, before, qkv, turn, triple, merger, expander, shrinker,
    t1, t2a, t2b, t3a, t3b, e1, e2a, e2b, e3a, e3b,
    up, act, ss, send, keep, bias, wide, merge, shrink, slopes, out, sems,
):
    shard, length = place[2], place[3]
    pairs = own_triple(shard, 0, triple, wide) + own_expander(shard, 0, expander, wide)
    pairs += first_triple(shard, (t1, t2a, t2b, t3a, t3b), wide)
    pairs += first_expander(shard, (e1, e2a, e2b, e3a, e3b), wide)
    started = copies(pairs + [(merger.at[0], merge), (shrinker.at[0], shrink)], sems)
    for k, u in enumerate((u0, u1, u2, u3)):
        up[pl.ds(k * 128, 128), :] = u[...]
    finish(started)
    for n in range(4):
        cols = pl.ds(n * 256, 256)
        value, slope = gelu_both(before[:, cols])
        act[:, cols] = value.astype(BF)
        ss[:, cols] = (dot_t(up[...], shrink[cols, :]) * slope).astype(BF)
    row, col = spots(shard)
    allowed = (col <= row) & (col < length)
    out[...] = dot_t(up[...], merge[...]).astype(BF)
    attend_back(qkv, allowed, None, out, slopes, False)
    triple_slopes(slopes, turn, ss)
    slopes_out(ss, bias, wide, send, keep)


def cut(at, d):
    return pl.ds(pl.multiple_of(((at + d) & 3) * 64, 64), 64)


def terms_a(place, act, up, normed, ss, a0, a1, a2, a3, term):
    x = place[0]
    for o in range(4):
        cols = pl.ds(o * 256, 256)
        term[:, pl.ds(0, W)] = t_dot(act[:, cols], up[...])
        term[:, pl.ds(W, 512)] = t_dot(normed[:, cols], ss[:, pl.ds(W, 512)])
        for d, ref in enumerate((a0, a1, a2, a3)):
            ref[pl.ds(o * 64, 64), :] = term[cut(x, d), :].astype(BF)


def terms_b(place, normed, ss, mixed, up, b0, b1, b2, b3, term, last):
    y = place[1]
    last[...] = t_dot(mixed[...], up[...])
    for o in range(4):
        cols = pl.ds(o * 256, 256)
        term[:, pl.ds(0, W)] = t_dot(normed[:, cols], ss[:, pl.ds(0, W)])
        term[:, pl.ds(W, 256)] = t_dot(normed[:, cols], ss[:, pl.ds(1536, 256)])
        for d, ref in enumerate((b0, b1, b2, b3)):
            ref[pl.ds(o * 64, 64), pl.ds(0, 1280)] = term[cut(y, d), :].astype(BF)
            ref[pl.ds(o * 64, 64), pl.ds(1280, 256)] = last[cut(y, d), cols].astype(BF)


def weight_terms(place, act, normed, up, ss, mixed):
    a = call(
        terms_a, [place, act, up, normed, ss], [SM] + [VM] * 4, [shape(256, CHUNK)] * 4,
        scratch=[pltpu.VMEM((256, CHUNK), F32)], flops=2 * 10**9,
    )
    b = call(
        terms_b, [place, normed, ss, mixed, up], [SM] + [VM] * 4, [shape(256, CHUNK)] * 4,
        scratch=[pltpu.VMEM((256, 1280), F32), pltpu.VMEM((256, W), F32)], flops=2 * 10**9,
    )
    return list(a), list(b)


def join(place, state, ak, ag, az, fk, fg, fz, vec, new, out, squares, *, layer):
    shard, length = place[2], place[3]
    spot = shard * 128 + lax.broadcasted_iota(jnp.int32, (128, 1), 0)
    valid = (spot < length).astype(F32)
    attended = ak[pl.ds(0, 128), :] + ag[pl.ds(0, 128), :].astype(F32) + az[...].astype(F32)
    attended = attended + vec[pl.ds(4 + layer, 1), :]
    branch = fk[pl.ds(0, 128), :] + fg[pl.ds(0, 128), :].astype(F32) + fz[...].astype(F32)
    branch = branch + vec[pl.ds(6 + layer, 1), :]
    old = state[...].astype(F32)
    for at, item in enumerate((old, attended, branch)):
        total = jnp.sum(jnp.sum(item * item, axis=1, keepdims=True) * valid)
        squares[pl.ds(at, 1), :] = jnp.full((1, 128), total, F32)
    state_new = old + attended + branch
    new[...] = state_new
    if layer == 0:
        hat, _ = normalize(state_new)
        out[...] = (hat * vec[pl.ds(1, 1), :] + vec[pl.ds(3, 1), :]).astype(BF)
    else:
        out[...] = (state_new * valid).astype(BF)


def norm_back(place, state, slope, up, sk, sg, sz, vec, new, low, rows, *, layer):
    shard, length = place[2], place[3]
    spot = shard * 128 + lax.broadcasted_iota(jnp.int32, (128, 1), 0)
    given = slope[...].astype(F32)
    upstream = up[...].astype(F32)
    if layer == LAYERS - 1:
        given = jnp.where(spot < length, given, 0.0)
        upstream = given
    sn = sk[pl.ds(0, 128), :] + sg[pl.ds(0, 128), :].astype(F32) + sz[...].astype(F32)
    hat, factor = normalize(state[...].astype(F32))
    rows[...] = jnp.zeros_like(rows)
    rows[pl.ds(0, 1), :] = jnp.sum(sn * hat, axis=0, keepdims=True)
    rows[pl.ds(1, 1), :] = jnp.sum(sn, axis=0, keepdims=True)
    rows[pl.ds(2, 1), :] = jnp.sum(upstream, axis=0, keepdims=True)
    d = sn * vec[pl.ds(layer, 1), :]
    mean = jnp.mean(d, axis=-1, keepdims=True)
    along = jnp.mean(d * hat, axis=-1, keepdims=True)
    result = given + factor * (d - mean - hat * along)
    new[...] = result
    low[...] = result.astype(BF)


def vectors_out(place, rows0, bias0, rows1, bias1, out, full):
    shard = place[2]
    full[...] = jnp.zeros_like(full)
    for at, (rows, bias) in enumerate(((rows0, bias0), (rows1, bias1))):
        base = at * 7
        full[pl.ds(base, 3), :] = rows[pl.ds(0, 3), :]
        for p in range(3):
            full[pl.ds(base + 3 + p, 1), lanes(shard * 256, 256)] = bias[
                pl.ds(0, 1), pl.ds(W + p * 256, 256)
            ]
        full[pl.ds(base + 6, 1), :] = bias[pl.ds(0, 1), pl.ds(0, W)]
    out[pl.ds(0, 16), :] = full[:, pl.ds(0, 512)]
    out[pl.ds(16, 16), :] = full[:, pl.ds(512, 512)]


def second_cut(place, own, r1, r2, r3, c0, c1, c2, c3, *, axis):
    at = place[axis]
    for o in range(4):
        for e, ref in enumerate((c0, c1, c2, c3)):
            rows = rows_at(o * 64 + ((at + e) & 3) * 16, 16)
            total = own[rows, :].astype(F32)
            for other in (r1, r2, r3):
                total = total + other[rows, :].astype(F32)
            ref[pl.ds(o * 16, 16), :] = total.astype(BF)


def z_send(place, a0, a1, a2, a3, b0, b1, b2, b3, vector, side, across, cross, plain, wide):
    shard = place[2]
    z_lo = shard >> 1
    a = a0[...].astype(F32) + a1[...].astype(F32) + a2[...].astype(F32) + a3[...].astype(F32)
    b = b0[...].astype(F32) + b1[...].astype(F32) + b2[...].astype(F32) + b3[...].astype(F32)
    wide[:, pl.ds(0, W)] = b[:, 0:W]
    wide[:, pl.ds(W, 512)] = a[:, W:CHUNK]
    wide[:, pl.ds(1536, 256)] = b[:, W:1280]
    plain[:, pl.ds(0, W)] = a[:, 0:W]
    plain[:, pl.ds(W, 256)] = b[:, 1280:CHUNK]
    cross[...] = wide[rows_at(z_lo * 32, 32), :]
    side[:, pl.ds(0, WIDE)] = wide[rows_at((1 - z_lo) * 32, 32), :].astype(BF)
    side[:, pl.ds(WIDE, 512)] = vector[...].astype(BF)
    across[:, pl.ds(0, WIDE)] = cross[...].astype(BF)
    across[:, pl.ds(WIDE, 1280)] = plain[pl.ds(0, 32), :].astype(BF)
    across[:, pl.ds(WIDE + 1280, 1280)] = plain[pl.ds(32, 32), :].astype(BF)
    across[:, pl.ds(WIDE + 2560, 512)] = vector[...].astype(BF)


def local_rows():
    row = lax.broadcasted_iota(jnp.int32, (32, 1), 0) & 15
    return (row == 6) | (row == 13)


def z_sum(place, cross, plain, vector, za, zb, z2, near, kept, whole, vec, both):
    core = place[2] & 1
    both[pl.ds(0, 32), :] = cross[...] + z2[:, pl.ds(0, WIDE)].astype(F32)
    both[pl.ds(32, 32), :] = za[:, pl.ds(0, WIDE)].astype(F32) + zb[:, pl.ds(0, WIDE)].astype(F32)
    for at in range(2):
        own = both[rows_at(at * 32 + core * 16, 16), :]
        other = both[rows_at(at * 32 + (1 - core) * 16, 16), :]
        kept[pl.ds(at * 16, 16), :] = own
        near[pl.ds(at * 16, 16), pl.ds(0, WIDE)] = other.astype(BF)
    for at in range(2):
        rows = pl.ds(at * 32, 32)
        got = z2[:, pl.ds(WIDE + at * 1280, 1280)].astype(F32)
        whole[rows, :] = (plain[rows, :] + got).astype(BF)
    sides = za[:, pl.ds(WIDE, 512)].astype(F32) + zb[:, pl.ds(WIDE, 512)].astype(F32)
    total = vector[...] + z2[:, pl.ds(WIDE + 2560, 512)].astype(F32)
    total = total + jnp.where(local_rows(), 0.0, sides)
    vec[...] = total
    near[:, pl.ds(WIDE, 512)] = total.astype(BF)


def payload(place, kept, near, whole, vec, a, b):
    shard = place[2]
    for k in range(4):
        rows = rows_at((shard ^ k) * 16, 16)
        ref, at = (near, k >> 1) if k & 1 else (kept, k >> 1)
        source = ref[pl.ds(at * 16, 16), pl.ds(0, WIDE)].astype(BF)
        b[rows, pl.ds(0, W)] = source[:, 0:W]
        a[rows, pl.ds(W, 512)] = source[:, W:1536]
        b[rows, pl.ds(W, 256)] = source[:, 1536:WIDE]
    a[pl.ds(0, 64), pl.ds(0, W)] = whole[:, pl.ds(0, W)]
    b[pl.ds(0, 64), pl.ds(1280, 256)] = whole[:, pl.ds(W, 256)]
    if a.shape[0] == 64:
        return
    total = vec[...] + jnp.where(local_rows(), 0.0, near[:, pl.ds(WIDE, 512)].astype(F32))
    low = total.astype(BF)
    a[pl.ds(64, 16), :] = jnp.zeros((16, CHUNK), BF)
    a[pl.ds(64, 16), pl.ds(0, 512)] = low[0:16]
    a[pl.ds(64, 16), pl.ds(512, 512)] = low[16:32]


def assemble(place, *refs, layer):
    a_refs, b_refs = refs[0:4], refs[4:8]
    refs = refs[8 + (4 if layer == 0 else 0) :]
    t_out, m_out, e_out, s_out, v_out, t, m, e, s, sems = refs
    x, y = place[0], place[1]
    started = []
    vector = jnp.zeros((16, W), F32)
    for d in range(4):
        for h in range(4):
            base = pl.multiple_of(((x + d) & 3) * 64 + ((y + h) & 3) * 16, 16)
            for o in range(4):
                value = a_refs[d][pl.ds(h * 64 + o * 16, 16), :].astype(F32)
                s[rows_at(o * 256 + base, 16), :] = value[:, 0:W]
                rows = pl.ds(base, 16)
                t[rows, pl.ds(o * 256, 256)] = value[:, W:1280]
                t[rows, pl.ds(W + o * 256, 256)] = value[:, 1280:CHUNK]
        if layer == 0:
            vector = vector + a_refs[d][pl.ds(256, 16), pl.ds(0, W)].astype(F32)
    started += copies([(s, s_out.at[layer])], sems)
    for d in range(4):
        for h in range(4):
            rows = pl.ds(pl.multiple_of(((y + d) & 3) * 64 + ((x + h) & 3) * 16, 16), 16)
            for o in range(4):
                value = b_refs[d][pl.ds(h * 64 + o * 16, 16), :].astype(F32)
                e[rows, pl.ds(o * W, W)] = value[:, 0:W]
                t[rows, pl.ds(2 * W + o * 256, 256)] = value[:, W:1280]
                m[rows, pl.ds(o * 256, 256)] = value[:, 1280:CHUNK]
    pairs = [(t, t_out.at[layer]), (m, m_out.at[layer]), (e, e_out.at[layer])]
    started += copies(pairs, sems.at[pl.ds(1, 3)])
    v_out[...] = vector
    finish(started)


def bundle(own, r1, r2, r3, out):
    for h, ref in enumerate((own, r1, r2, r3)):
        out[pl.ds(h * 64, 64), :] = ref[pl.ds(0, 64), :]
    if out.shape[0] > 256:
        rows = pl.ds(64, 16)
        total = own[rows, :].astype(F32) + r1[rows, :].astype(F32)
        total = total + r2[rows, :].astype(F32) + r3[rows, :].astype(F32)
        out[pl.ds(256, 16), :] = total.astype(BF)


def sum_over_reps(place, start, a, b, vector, layer, earlier):
    def exchange(chunks, axis):
        return [chunks[0]] + [step(chunks[d], axis, d) for d in (1, 2, 3)]

    a = exchange(a, 0)
    b = exchange(b, 1)
    chunk = [shape(64, CHUNK)] * 4
    a = call(functools.partial(second_cut, axis=1), [start] + a, [SM] + [VM] * 4, chunk)
    b = call(functools.partial(second_cut, axis=0), [start] + b, [SM] + [VM] * 4, chunk)
    a = exchange(a, 1)
    b = exchange(b, 0)
    side, across, cross, plain = call(
        z_send, [place] + a + b + [vector], [SM] + [VM] * 9,
        [shape(32, 2304), shape(32, 4864), shape(32, WIDE, dtype=F32), shape(64, 1280, dtype=F32)],
        scratch=[pltpu.VMEM((64, WIDE), F32)],
    )
    z2 = move(across, flip_z=2)
    za = move(side, flip_z=1)
    zb = move(side, flip_z=3)
    near, kept, whole, vec = call(
        z_sum, [place, cross, plain, vector, za, zb, z2], [SM] + [VM] * 6,
        [shape(32, 2304), shape(32, WIDE, dtype=F32), shape(64, 1280), shape(32, 512, dtype=F32)],
        scratch=[pltpu.VMEM((64, WIDE), F32)],
    )
    near = move(near, flip_core=1)
    a, b = call(
        payload, [place, kept, near, whole, vec], [SM] + [VM] * 4,
        [shape(64 if layer else 80, CHUNK), shape(64, CHUNK)],
    )

    def collect(own, axis):
        return [own] + [step(own, axis, -d) for d in (1, 2, 3)]

    (a,) = call(bundle, collect(a, 1), [VM] * 4, [shape(256 if layer else 272, CHUNK)])
    (b,) = call(bundle, collect(b, 0), [VM] * 4, [shape(256, CHUNK)])
    a = collect(a, 0)
    b = collect(b, 1)
    outs = [
        shape(LAYERS, 256, 3072, dtype=F32),
        shape(LAYERS, 256, 1024, dtype=F32),
        shape(LAYERS, 256, 4096, dtype=F32),
        shape(LAYERS, 1024, 1024, dtype=F32),
        shape(16, W, dtype=F32),
    ]
    args, specs = [place] + a + b, [SM] + [VM] * 8
    aliases = {}
    if layer == 0:
        args, specs = args + list(earlier), specs + [ANY] * 4
        aliases = {9 + i: i for i in range(4)}
    return call(
        functools.partial(assemble, layer=layer), args, specs, outs, out_specs=[ANY] * 4 + [VM],
        scratch=[
            pltpu.VMEM((256, 3072), F32),
            pltpu.VMEM((256, 1024), F32),
            pltpu.VMEM((256, 4096), F32),
            pltpu.VMEM((1024, 1024), F32),
            pltpu.SemaphoreType.DMA((4,)),
        ],
        aliases=aliases,
    )


def gather_tokens(own):
    far = move(own, flip_z=1)
    near = move(own, flip_core=1)
    return [own, near, far, move(far, flip_core=1)]


def body(
    inputs,
    lengths,
    gains,
    shifts,
    triple,
    triple_bias,
    merger,
    merger_bias,
    expander,
    expander_bias,
    shrinker,
    shrinker_bias,
    cotangent,
):
    rep = lax.axis_index("rep")
    shard = lax.axis_index("shard")
    length = lengths[0]
    place = jnp.stack([rep // 8, rep % 4, shard, length]).astype(jnp.int32)

    pieces = call(
        cut_triple, [place, triple], [SM, ANY], [shape(256, 768)] + [shape(128, 768)] * 4,
        scratch=[pltpu.VMEM((256, 3072), BF), pltpu.SemaphoreType.DMA((1,))],
    )
    x_blocks = gather_tokens(inputs)
    small = jnp.concatenate(
        [v.reshape(-1, 256) for v in (gains, shifts, merger_bias, shrinker_bias, triple_bias)]
    )
    small = [small] + [move(small, flip_z=k >> 1, flip_core=k & 1) for k in (1, 2, 3)]

    def halves(cut):
        return [
            move(cut[0], flip_core=1),
            move(cut[1], flip_z=1),
            move(cut[2], flip_z=3),
            move(cut[3], flip_z=1, flip_core=1),
            move(cut[4], flip_z=3, flip_core=1),
        ]

    t_pieces = halves(pieces)
    cut = call(
        cut_rest, [after(place, pieces[0]), triple, expander], [SM, ANY, ANY],
        [shape(256, W)] + [shape(128, W)] * 4 + [shape(256, WIDE)] * 3,
        scratch=[
            pltpu.VMEM((256, 3072), BF), pltpu.VMEM((256, 4096), BF), pltpu.VMEM((256, 4096), BF),
            pltpu.SemaphoreType.DMA((3,)),
        ],
    )
    e_pieces = halves(after(tuple(cut[:5]), t_pieces[2], t_pieces[4]))
    rest = after(tuple(cut[5:]), e_pieces[2], e_pieces[4])
    w_pieces = [
        move(rest[0], flip_core=1),
        move(rest[1], flip_z=3),
        move(rest[2], flip_z=3, flip_core=1),
    ]
    up_blocks = gather_tokens(after(cotangent, e_pieces[1], e_pieces[3]))

    lined = jnp.stack([pick(jnp.stack(small), shard ^ j) for j in range(4)]).astype(F32)
    triple_rows = lined[:, 8:14].reshape(4, LAYERS, 3, 256).transpose(1, 0, 2, 3)
    triple_rows = pick(triple_rows.reshape(LAYERS, 3, 4, 256), shard, 2).reshape(LAYERS, 768)
    vec = jnp.concatenate(
        [
            lined[:, :8].transpose(1, 0, 2).reshape(8, W),
            jnp.pad(triple_rows, ((0, 0), (0, 256))),
            expander_bias.astype(F32),
        ]
    )
    spot = jnp.arange(512, dtype=jnp.int32)
    spot = (((spot >> 7) ^ shard) << 7) | (spot & 127)
    index = jnp.arange(ROT // 2, dtype=F32)
    freq = jnp.exp(index * (-2.0 * math.log(10000.0) / ROT))
    lane = jnp.arange(256, dtype=jnp.int32) % HD
    phase = spot.astype(F32)[:, None] * jnp.tile(freq, 16)[None, :]
    cosine, sine = jnp.cos(phase), jnp.sin(phase)
    turn = jnp.stack(
        [
            jnp.where(lane < ROT, cosine, 1.0),
            jnp.where(lane < ROT // 2, -sine, 0.0),
            jnp.where((lane >= ROT // 2) & (lane < ROT), sine, 0.0),
        ]
    )

    full = shape(512, W)
    send, keep = shape(256, W), shape(256, W, dtype=F32)
    wide = pltpu.VMEM((W, WIDE), BF)
    merge, shrink = pltpu.VMEM((256, W), BF), pltpu.VMEM((W, W), BF)

    normed0, qkv0, mixed0, a_send, a_keep = call(
        first_attention,
        [place] + x_blocks + [vec, turn, triple, merger] + t_pieces,
        [SM] + [VM] * 6 + [ANY] * 7,
        [full, shape(512, 768), shape(512, 256), send, keep],
        scratch=[wide, merge, pltpu.SemaphoreType.DMA((9,))],
        flops=2 * 10**9,
    )
    a_got = move(a_send, flip_core=1)
    before0, f_send, f_keep = call(
        first_forward,
        [place, normed0, vec, expander, shrinker] + e_pieces,
        [SM, VM, VM] + [ANY] * 7,
        [shape(512, W, dtype=F32), send, keep],
        scratch=[wide, shrink, pltpu.VMEM((512, W), BF), pltpu.SemaphoreType.DMA((7,))],
        flops=2 * 10**9,
    )
    f_got = move(f_send, flip_core=1)

    def other(kept, got):
        return move((kept[128:] + got[128:].astype(F32)).astype(BF), flip_z=1)

    sums = [a_keep, a_got, other(a_keep, a_got), f_keep, f_got, other(f_keep, f_got)]
    block = [shape(128, W, dtype=F32), shape(128, W), shape(8, 128, dtype=F32)]
    state1, normed1, squares0 = call(
        functools.partial(join, layer=0), [place, inputs] + sums + [vec], [SM] + [VM] * 8, block
    )
    n_blocks = gather_tokens(normed1)

    (normed1, up1, act1, ss1, mixed1, a_send, a_keep, f_send, f_keep, send1, keep1, bias1) = call(
        last_layer,
        [place] + n_blocks + up_blocks + [vec, turn, triple, merger, expander, shrinker] + w_pieces,
        [SM] + [VM] * 10 + [ANY] * 7,
        [full, full, full, shape(512, WIDE), shape(512, 256)]
        + [send, keep] * 3
        + [shape(8, WIDE, dtype=F32)],
        scratch=[
            wide, merge, shrink, pltpu.VMEM((512, 768), BF), pltpu.VMEM((512, 768), F32),
            pltpu.VMEM((512, 256), BF), pltpu.VMEM((512, W), F32), pltpu.SemaphoreType.DMA((9,)),
        ],
        flops=8 * 10**9,
    )
    got1 = move(send1, flip_core=1)
    far1 = other(keep1, got1)
    a1, b1 = weight_terms(place, act1, normed1, up1, ss1, mixed1)
    slope1, low1, rows1 = call(
        functools.partial(norm_back, layer=1),
        [place, state1, cotangent, cotangent, keep1, got1, far1, vec],
        [SM] + [VM] * 7,
        [shape(128, W, dtype=F32), shape(128, W), shape(8, W, dtype=F32)],
    )
    u_blocks = gather_tokens(low1)
    a_got = move(a_send, flip_core=1)
    f_got = move(f_send, flip_core=1)
    sums = [a_keep, a_got, other(a_keep, a_got), f_keep, f_got, other(f_keep, f_got)]
    _, hidden_out, squares1 = call(
        functools.partial(join, layer=1), [place, state1] + sums + [vec], [SM] + [VM] * 8, block
    )

    up0, act0, ss0, send0, keep0, bias0 = call(
        first_back,
        [place] + u_blocks + [before0, qkv0, turn, triple, merger, expander, shrinker]
        + t_pieces + e_pieces,
        [SM] + [VM] * 7 + [ANY] * 14,
        [full, full, shape(512, WIDE), send, keep, shape(8, WIDE, dtype=F32)],
        scratch=[
            wide, merge, shrink, pltpu.VMEM((512, 768), F32), pltpu.VMEM((512, 256), BF),
            pltpu.SemaphoreType.DMA((16,)),
        ],
        flops=5 * 10**9,
    )
    *sums1, _ = sum_over_reps(place, after(place, up0), a1, b1, jnp.zeros((32, 512), F32), 1, None)
    a0, b0 = weight_terms(place, act0, normed0, up0, ss0, mixed0)
    got0 = move(send0, flip_core=1)
    far0 = other(keep0, got0)
    input_grad, _, rows0 = call(
        functools.partial(norm_back, layer=0),
        [place, inputs, slope1, low1, keep0, got0, far0, vec],
        [SM] + [VM] * 7,
        [shape(128, W, dtype=F32), shape(128, W), shape(8, W, dtype=F32)],
    )
    (vector,) = call(
        vectors_out, [place, rows0, bias0, rows1, bias1], [SM] + [VM] * 4,
        [shape(32, 512, dtype=F32)], scratch=[pltpu.VMEM((16, W), F32)],
    )
    *sums0, summed = sum_over_reps(place, place, a0, b0, vector, 0, sums1)

    totals = jnp.concatenate([squares0[:3, :1], squares1[:3, :1]]).reshape(1, 6)
    totals = totals + move(totals, flip_core=1)
    totals = totals + move(totals, flip_z=1)
    rms_stats = jnp.sqrt(totals / (length.astype(F32) * W) + 1e-06)

    def vector_of(row, count):
        both = jnp.stack([summed[row : row + count], summed[row + 7 : row + 7 + count]])
        return pick(both.reshape(LAYERS, 4, -1), shard, 1)

    bias_part = vector_of(2, 1)
    return (
        hidden_out,
        input_grad,
        vector_of(0, 1),
        vector_of(1, 1),
        sums0[0],
        vector_of(3, 3),
        sums0[1],
        bias_part,
        sums0[2],
        jnp.stack([summed[6], summed[13]]),
        sums0[3],
        bias_part,
        rms_stats,
    )


def solution(mesh):
    return jax.shard_map(
        body,
        mesh=mesh,
        in_specs=(
            P(("rep", "shard"), None),
            P("rep"),
            P(None, "shard"),
            P(None, "shard"),
            P(None, "shard", None),
            P(None, "shard"),
            P(None, "shard", None),
            P(None, "shard"),
            P(None, "shard", None),
            P(None, "shard"),
            P(None, "shard", None),
            P(None, "shard"),
            P(("rep", "shard"), None),
        ),
        out_specs=(
            P(("rep", "shard"), None),
            P(("rep", "shard"), None),
            P(None, "shard"),
            P(None, "shard"),
            P(None, "shard", None),
            P(None, "shard"),
            P(None, "shard", None),
            P(None, "shard"),
            P(None, "shard", None),
            P(None, "shard"),
            P(None, "shard", None),
            P(None, "shard"),
            P("rep", None),
        ),
        check_vma=False,
    )
```

time: 1730 us -> 471 us (0.27)
  waiting for transfers between devices: 1200 us -> 180 us
  blocking collectives: 267 us -> 0 us
  Pallas kernels: 0 us -> 154 us
  matrix products: 147 us -> 0 us
  starting transfers between devices: 2.51 us -> 101 us
  local copies, waits for them, and re-layouts: 55.7 us -> 17.1 us
  other arithmetic: 33.3 us -> 7.2 us
    reduce_scatter x8 -> x0, waiting for transfers between devices: 499 us -> none  [the longest x2 166 us: body(): lax.psum_scatter(expander_slope.astype(jnp.bfloat16), 'shard', scatter_di...]
    all_gather x12 -> x0, waiting for transfers between devices: 487 us -> none  [the longest x2 158 us: body(): lax.all_gather(shrinker[layer], 'shard', axis=0, tiled=True)]
    psum x2 -> x0, blocking collectives: 190 us -> none  [the longest x1 183 us: body(): lax.psum(owned[0].astype(jnp.bfloat16), 'rep').astype(jnp.float32)]
    psum x1 -> x0, waiting for transfers between devices: 183 us -> none  [body(): lax.psum(owned[2].astype(jnp.bfloat16), 'rep').astype(jnp.float32)]
    ppermute x0 -> x98, waiting for transfers between devices: none -> 180 us  [move(): return lax.ppermute(value, AXES, pairs)]
    pallas_call x0 -> x31, Pallas kernels: none -> 154 us  [call(): pl.pallas_call(body, out_shape=outs, in_specs=specs, out_specs=out_specs...]
    dot_general x36 -> x0, matrix products: 147 us -> none  [the longest x2 15.8 us: body(): jnp.dot(upstream, shrinker_full.T, preferred_element_type=jnp.float32)]
    ppermute x0 -> x98, starting transfers between devices: none -> 101 us  [move(): return lax.ppermute(value, AXES, pairs)]
  transfers between devices with their start and end apart: 25 -> 98, of which waited for: 22 -> 32; matrix products, arithmetic and copies ran while one was open for 10% -> 2% of each run, Pallas kernels for 0% -> 27%
where the time goes in v1:
time: 471 us; the launch traced here: 462 us
  waiting for transfers between devices  180 us (38%)
  Pallas kernels  154 us (33%)
  starting transfers between devices  101 us (21%)
  local copies, waits for them, and re-layouts  17.1 us (4%)
  other arithmetic  7.2 us (2%)
    ppermute x98, waiting for transfers between devices, move(): return lax.ppermute(value, AXES, pairs)  180 us
    pallas_call x31, Pallas kernels, call(): pl.pallas_call(body, out_shape=outs, in_specs=specs, out_specs=out_specs...  154 us
    ppermute x98, starting transfers between devices, move(): return lax.ppermute(value, AXES, pairs)  101 us
    unnamed x233, local copies, waits for them, and re-layouts  12 us
  transfers between devices with their start and end apart: 98, of which 32 were waited for; matrix products, arithmetic and copies ran while one was open for 2% of the time, Pallas kernels for 27%

profile of v1, /device:TPU:0, one launch (start us, length us, event | category | flops | bytes accessed | tf_op | source)
XLA Modules:
  0.0 462.1 jit_solution(12482187158983349670)
XLA Ops:
  7.3 3.2 shard_map.228
  10.5 2.6 collective-permute-start.8
  16.5 5.8 %shard_map.230 = (bf16[256,1024]{1,0:T(8,128)(2,1)}, bf16[128,1024]{1,0:T(8,128)(2,1)}, bf16[128,1024]{1,0:T(8,128)(2,1)}, bf16[128,1024]{1,0:T(8,128)(2,1)}, bf...) custom-call(s32[4]{0:T(128)} %pad_add_fusion.place, ...), custom_call_target="tpu_custom_call" | custom-call | bytes 4325376 | tf_op jit(solution)/shard_map/pallas_call | solution.py:68
  24.6 7.0 %collective-permute-done.10.t3b = bf16[128,768]{1,0:T(8,128)(2,1)S(1)} collective-permute-done((bf16[128,768]{1,0:T(8,128)(2,1)S(1)}, bf16[128,768]{1,0:T(8,128)(2,1)S(1)}, u32[]{:S(2)}, u32[]{:S(2)}) %collective-permute-start.10) | collective-permute-done | bytes 196640 | tf_op jit(solution)/shard_map/ppermute | solution.py:46
  32.0 6.5 %collective-permute-done.9.t3a = bf16[128,768]{1,0:T(8,128)(2,1)S(1)} collective-permute-done((bf16[128,768]{1,0:T(8,128)(2,1)S(1)}, bf16[128,768]{1,0:T(8,128)(2,1)S(1)}, u32[]{:S(2)}, u32[]{:S(2)}) %collective-permute-start.9) | collective-permute-done | bytes 196640 | tf_op jit(solution)/shard_map/ppermute | solution.py:46
  40.1 2.9 collective-permute-start.17
  43.8 8.7 %shard_map.229 = (bf16[512,1024]{1,0:T(8,128)(2,1)}, bf16[512,768]{1,0:T(8,128)(2,1)}, bf16[512,256]{1,0:T(8,128)(2,1)}, bf16[256,1024]{1,0:T(8,128)(2,1)}, f32[256,1024]{1,0:T(8,128)}) custom-call(s32[4]{0:T(128)} %pad_add_fusion.place, bf16[128,1024]{1,0:T(8,128)(2,1)} %state.3, bf16[128,1024]{1,0:T(8,128)(2,1)} %copy-done.54, ...), custom_call_target="tpu_custom_call" | custom-call | flops 2000000000 | bytes 6340608 | tf_op jit(solution)/shard_map/pallas_call | solution.py:68
  54.2 7.5 %shard_map.231 = (f32[512,1024]{1,0:T(8,128)}, bf16[256,1024]{1,0:T(8,128)(2,1)}, f32[256,1024]{1,0:T(8,128)}) custom-call(s32[4]{0:T(128)} %pad_add_fusion.place, bf16[512,1024]{1,0:T(8,128)(2,1)} %get-tuple-element.141.normed, f32[12,1024]{1,0:T(8,128)} %fusion.4.vec, bf16[2,256,4096]{2,1,0:T(8,128)(2,1)} %expander.7, bf16[2,1024,1024]{2,1,0:T(8,128)(2,1)} %shrinker.5, ...), custom_call_target="tpu_custom_call" | custom-call | flops 2000000000 | bytes 4767744 | tf_op jit(solution)/shard_map/pallas_call | solution.py:68
  65.3 2.4 collective-permute-start.28
  68.8 2.7 collective-permute-done.24.u2
  72.0 5.2 %collective-permute-done.12.az = bf16[128,1024]{1,0:T(8,128)(2,1)S(1)} collective-permute-done((bf16[128,1024]{1,0:T(8,128)(2,1)S(1)}, bf16[128,1024]{1,0:T(8,128)(2,1)S(1)}, u32[]{:S(2)}, u32[]{:S(2)}) %collective-permute-start.12) | collective-permute-done | bytes 262176 | tf_op jit(solution)/shard_map/ppermute | solution.py:46
  77.2 4.8 %collective-permute-done.19.fz = bf16[128,1024]{1,0:T(8,128)(2,1)S(1)} collective-permute-done((bf16[128,1024]{1,0:T(8,128)(2,1)S(1)}, bf16[128,1024]{1,0:T(8,128)(2,1)S(1)}, u32[]{:S(2)}, u32[]{:S(2)}) %collective-permute-start.19) | collective-permute-done | bytes 262176 | tf_op jit(solution)/shard_map/ppermute | solution.py:46
  82.6 3.3 shard_map.232
  86.5 7.8 %collective-permute-done.21.n2 = bf16[128,1024]{1,0:T(8,128)(2,1)S(1)} collective-permute-done((bf16[128,1024]{1,0:T(8,128)(2,1)}, bf16[128,1024]{1,0:T(8,128)(2,1)S(1)}, u32[]{:S(2)}, u32[]{:S(2)}) %collective-permute-start.21) | collective-permute-done | bytes 262176 | tf_op jit(solution)/shard_map/ppermute | solution.py:46
  94.6 13.3 %collective-permute-done.28.w3 = bf16[256,1792]{1,0:T(8,128)(2,1)} collective-permute-done((bf16[256,1792]{1,0:T(8,128)(2,1)S(1)}, bf16[256,1792]{1,0:T(8,128)(2,1)}, u32[]{:S(2)}, u32[]{:S(2)}) %collective-permute-start.28) | collective-permute-done | bytes 917536 | tf_op jit(solution)/shard_map/ppermute | solution.py:46
  109.3 19.7 %shard_map.233 = (bf16[512,1024]{1,0:T(8,128)(2,1)}, bf16[512,1024]{1,0:T(8,128)(2,1)}, bf16[512,1024]{1,0:T(8,128)(2,1)}, bf16[512,1792]{1,0:T(8,128)(2,1)}, bf...) custom-call(s32[4]{0:T(128)} %pad_add_fusion.place, ...), custom_call_target="tpu_custom_call" | custom-call | flops 8000000000 | bytes 13737984 | tf_op jit(solution)/shard_map/pallas_call | solution.py:68
  129.8 6.6 %shard_map.248 = (bf16[256,1536]{1,0:T(8,128)(2,1)}, bf16[256,1536]{1,0:T(8,128)(2,1)}, bf16[256,1536]{1,0:T(8,128)(2,1)}, bf16[256,1536]{1,0:T(8,128)(2,1)}) custom-call(s32[4]{0:T(128)} %pad_add_fusion.place, bf16[512,1024]{1,0:T(8,128)(2,1)} %get-tuple-element.213.act, bf16[512,1024]{1,0:T(8,128)(2,1)} %get-tuple-element.214.up, ...), custom_call_target="tpu_custom_call" | custom-call | flops 2000000000 | bytes 8126464 | tf_op jit(solution)/shard_map/pallas_call | solution.py:68
  138.1 8.1 %collective-permute-done.34.sz = bf16[128,1024]{1,0:T(8,128)(2,1)S(1)} collective-permute-done((bf16[128,1024]{1,0:T(8,128)(2,1)S(1)}, bf16[128,1024]{1,0:T(8,128)(2,1)S(1)}, u32[]{:S(2)}, u32[]{:S(2)}) %collective-permute-start.34) | collective-permute-done | bytes 262176 | tf_op jit(solution)/shard_map/ppermute | solution.py:46
  146.9 3.2 shard_map.235
  150.5 7.2 %collective-permute-done.36.u2 = bf16[128,1024]{1,0:T(8,128)(2,1)S(1)} collective-permute-done((bf16[128,1024]{1,0:T(8,128)(2,1)}, bf16[128,1024]{1,0:T(8,128)(2,1)S(1)}, u32[]{:S(2)}, u32[]{:S(2)}) %collective-permute-start.36) | collective-permute-done | bytes 262176 | tf_op jit(solution)/shard_map/ppermute | solution.py:46
  157.7 2.8 collective-permute-start.69
  161.9 6.3 %shard_map.250 = (bf16[256,1536]{1,0:T(8,128)(2,1)}, bf16[256,1536]{1,0:T(8,128)(2,1)}, bf16[256,1536]{1,0:T(8,128)(2,1)}, bf16[256,1536]{1,0:T(8,128)(2,1)}) custom-call(s32[4]{0:T(128)} %pad_add_fusion.place, bf16[512,1024]{1,0:T(8,128)(2,1)} %get-tuple-element.215.normed, bf16[512,1792]{1,0:T(8,128)(2,1)} %get-tuple-element.216.ss, ...), custom_call_target="tpu_custom_call" | custom-call | flops 2000000000 | bytes 7340032 | tf_op jit(solution)/shard_map/pallas_call | solution.py:68
  169.9 2.9 collective-permute-start.75
  174.3 15.8 %shard_map.236 = (bf16[512,1024]{1,0:T(8,128)(2,1)}, bf16[512,1024]{1,0:T(8,128)(2,1)}, bf16[512,1792]{1,0:T(8,128)(2,1)}, bf16[256,1024]{1,0:T(8,128)(2,1)}, f32[256,1024]{1,0:T(8,128)}, /*index=5*/f32[8,1792]{1,0:T(8,128)}) custom-call(s32[4]{0:T(128)} %pad_add_fusion.place, bf16[128,1024]{1,0:T(8,128)(2,1)} %get-tuple-element.172.u0.up, ...), custom_call_target="tpu_custom_call" | custom-call | flops 5000000000 | bytes 11067392 | tf_op jit(solution)/shard_map/pallas_call | solution.py:68
  190.1 5.0 %collective-permute-done.70.r3 = bf16[256,1536]{1,0:T(8,128)(2,1)S(1)} collective-permute-done((bf16[256,1536]{1,0:T(8,128)(2,1)S(1)}, bf16[256,1536]{1,0:T(8,128)(2,1)S(1)}, u32[]{:S(2)}, u32[]{:S(2)}) %collective-permute-start.70) | collective-permute-done | bytes 786464 | tf_op jit(solution)/shard_map/ppermute | solution.py:46
  196.0 3.0 shard_map.249
  200.6 2.9 collective-permute-start.72
  204.9 3.4 collective-permute-done.75.r2
  209.4 3.0 shard_map.251
  213.4 2.5 collective-permute-start.79
  216.0 6.6 %shard_map.238 = (bf16[256,1536]{1,0:T(8,128)(2,1)}, bf16[256,1536]{1,0:T(8,128)(2,1)}, bf16[256,1536]{1,0:T(8,128)(2,1)}, bf16[256,1536]{1,0:T(8,128)(2,1)}) custom-call(s32[4]{0:T(128)} %pad_add_fusion.place, bf16[512,1024]{1,0:T(8,128)(2,1)} %get-tuple-element.178.act, bf16[512,1024]{1,0:T(8,128)(2,1)} %get-tuple-element.179.up, ...), custom_call_target="tpu_custom_call" | custom-call | flops 2000000000 | bytes 8126464 | tf_op jit(solution)/shard_map/pallas_call | solution.py:68
  224.4 2.7 shard_map.252
  227.8 4.0 collective-permute-start.82
  231.8 3.0 collective-permute-done.81.zb
  237.0 5.7 %collective-permute-done.82.z2 = bf16[32,4864]{1,0:T(8,128)(2,1)S(1)} collective-permute-done((bf16[32,4864]{1,0:T(8,128)(2,1)}, bf16[32,4864]{1,0:T(8,128)(2,1)S(1)}, u32[]{:S(2)}, u32[]{:S(2)}) %collective-permute-start.82) | collective-permute-done | bytes 311328 | tf_op jit(solution)/shard_map/ppermute | solution.py:46
  242.7 2.4 collective-permute-start.42
  247.5 6.4 %shard_map.240 = (bf16[256,1536]{1,0:T(8,128)(2,1)}, bf16[256,1536]{1,0:T(8,128)(2,1)}, bf16[256,1536]{1,0:T(8,128)(2,1)}, bf16[256,1536]{1,0:T(8,128)(2,1)}) custom-call(s32[4]{0:T(128)} %pad_add_fusion.place, bf16[512,1024]{1,0:T(8,128)(2,1)} %get-tuple-element.141.normed, bf16[512,1792]{1,0:T(8,128)(2,1)} %get-tuple-element.180.ss, ...), custom_call_target="tpu_custom_call" | custom-call | flops 2000000000 | bytes 7340032 | tf_op jit(solution)/shard_map/pallas_call | solution.py:68
  253.8 3.9 collective-permute-start.46
  258.8 3.0 collective-permute-start.48
  261.8 10.5 %collective-permute-done.42.r3 = bf16[256,1536]{1,0:T(8,128)(2,1)S(1)} collective-permute-done((bf16[256,1536]{1,0:T(8,128)(2,1)}, bf16[256,1536]{1,0:T(8,128)(2,1)S(1)}, u32[]{:S(2)}, u32[]{:S(2)}) %collective-permute-start.42) | collective-permute-done | bytes 786464 | tf_op jit(solution)/shard_map/ppermute | solution.py:46
  274.5 3.1 shard_map.239
  279.9 2.5 collective-permute-start.91
  282.5 3.0 collective-permute-start.90
  285.4 8.2 %collective-permute-done.47.r2 = bf16[256,1536]{1,0:T(8,128)(2,1)S(1)} collective-permute-done((bf16[256,1536]{1,0:T(8,128)(2,1)}, bf16[256,1536]{1,0:T(8,128)(2,1)S(1)}, u32[]{:S(2)}, u32[]{:S(2)}) %collective-permute-start.47) | collective-permute-done | bytes 786464 | tf_op jit(solution)/shard_map/ppermute | solution.py:46
  293.7 3.4 collective-permute-start.44
  297.2 3.1 shard_map.241
  302.7 3.1 collective-permute-done.43.a1
  311.1 3.0 collective-permute-done.49.b1
  315.9 3.2 shard_map.237
  321.3 2.7 shard_map.243
  325.8 2.6 collective-permute-start.53
  329.1 3.4 shard_map.234
  340.5 2.9 collective-permute-done.97
  348.2 7.8 %collective-permute-done.86.r3 = bf16[64,1536]{1,0:T(8,128)(2,1)S(1)} collective-permute-done((bf16[64,1536]{1,0:T(8,128)(2,1)S(1)}, bf16[64,1536]{1,0:T(8,128)(2,1)S(1)}, u32[]{:S(2)}, u32[]{:S(2)}) %collective-permute-start.86) | collective-permute-done | bytes 196640 | tf_op jit(solution)/shard_map/ppermute | solution.py:46
  358.5 2.5 collective-permute-start.56
  361.0 7.3 %collective-permute-done.64.r3 = bf16[64,1536]{1,0:T(8,128)(2,1)S(1)} collective-permute-done((bf16[64,1536]{1,0:T(8,128)(2,1)}, bf16[64,1536]{1,0:T(8,128)(2,1)S(1)}, u32[]{:S(2)}, u32[]{:S(2)}) %collective-permute-start.64) | collective-permute-done | bytes 196640 | tf_op jit(solution)/shard_map/ppermute | solution.py:46
  370.7 3.9 collective-permute-done.62.r1
  374.6 2.9 collective-permute-start.88
  383.1 6.3 %collective-permute-done.93.refs_5_ = bf16[256,1536]{1,0:T(8,128)(2,1)S(1)} collective-permute-done((bf16[256,1536]{1,0:T(8,128)(2,1)S(1)}, bf16[256,1536]{1,0:T(8,128)(2,1)S(1)}, u32[]{:S(2)}, u32[]{:S(2)}) %collective-permute-start.93) | collective-permute-done | bytes 786464 | tf_op jit(solution)/shard_map/ppermute | solution.py:46
  391.4 20.9 %collective-permute-done.89.refs_3_ = bf16[256,1536]{1,0:T(8,128)(2,1)S(1)} collective-permute-done((bf16[256,1536]{1,0:T(8,128)(2,1)}, bf16[256,1536]{1,0:T(8,128)(2,1)S(1)}, u32[]{:S(2)}, u32[]{:S(2)}) %collective-permute-start.89) | collective-permute-done | bytes 786464 | tf_op jit(solution)/shard_map/ppermute | solution.py:46
  415.7 8.8 %shard_map.257 = (f32[2,256,3072]{2,1,0:T(8,128)}, f32[2,256,1024]{2,1,0:T(8,128)}, f32[2,256,4096]{2,1,0:T(8,128)}, f32[2,1024,1024]{2,1,0:T(8,128)}, f32[16,1024]{1,0:T(8,128)}) custom-call(s32[4]{0:T(128)} %pad_add_fusion.place, bf16[256,1536]{1,0:T(8,128)(2,1)} %shard_map.255.refs_0_, bf16[256,1536]{1,0:T(8,128)(2,1)} %collective-permute-done.87.refs_1_, ...), custom_call_target="tpu_custom_call" | custom-call | bytes 31522816 | tf_op jit(solution)/shard_map/pallas_call | solution.py:68
  424.6 9.3 %collective-permute-done.66.refs_6_ = bf16[256,1536]{1,0:T(8,128)(2,1)S(1)} collective-permute-done((bf16[256,1536]{1,0:T(8,128)(2,1)}, bf16[256,1536]{1,0:T(8,128)(2,1)S(1)}, u32[]{:S(2)}, u32[]{:S(2)}) %collective-permute-start.66) | collective-permute-done | bytes 786464 | tf_op jit(solution)/shard_map/ppermute | solution.py:46
  433.8 11.8 %collective-permute-done.65.refs_5_ = bf16[256,1536]{1,0:T(8,128)(2,1)S(1)} collective-permute-done((bf16[256,1536]{1,0:T(8,128)(2,1)}, bf16[256,1536]{1,0:T(8,128)(2,1)S(1)}, u32[]{:S(2)}, u32[]{:S(2)}) %collective-permute-start.65) | collective-permute-done | bytes 786464 | tf_op jit(solution)/shard_map/ppermute | solution.py:46
  448.1 8.9 %shard_map.258 = (f32[2,256,3072]{2,1,0:T(8,128)}, f32[2,256,1024]{2,1,0:T(8,128)}, f32[2,256,4096]{2,1,0:T(8,128)}, f32[2,1024,1024]{2,1,0:T(8,128)}, f32[16,1024]{1,0:T(8,128)}) custom-call(s32[4]{0:T(128)} %pad_add_fusion.place, bf16[272,1536]{1,0:T(8,128)(2,1)} %shard_map.246.refs_0_, ...), custom_call_target="tpu_custom_call", output_to_operand_aliasing={{0}: (9, {}), {1}: (10, {}), {2}: (11, {}), {3}: (12, {})} | custom-call | bytes 31719424 | tf_op jit(solution)/shard_map/pallas_call | solution.py:68
  (446 shorter events, 100.2 us)
Async XLA Ops:
  2.1 20.3 %collective-permute-start.5 = (bf16[14,256]{1,0:T(8,128)(2,1)S(1)}, bf16[14,256]{1,0:T(8,128)(2,1)S(1)}, u32[]{:S(2)}, u32[]{:S(2)}) collective-permute-start(bf16[14,256]{1,0:T(8,128)(2,1)S(1)} %concatenate.13), channel_id=1, source_target_pairs={{0,3},{1,2},{2,1},{3,0},{4,7},{5,6},{6,5},{7,4},{8,11},{9,10},{10,... | collective-permute-start | bytes 21512 | tf_op jit(solution)/shard_map/ppermute | solution.py:46
  3.6 18.9 %collective-permute-start.4 = (bf16[14,256]{1,0:T(8,128)(2,1)S(1)}, bf16[14,256]{1,0:T(8,128)(2,1)S(1)}, u32[]{:S(2)}, u32[]{:S(2)}) collective-permute-start(bf16[14,256]{1,0:T(8,128)(2,1)S(1)} %concatenate.13), channel_id=1, source_target_pairs={{0,2},{1,3},{2,0},{3,1},{4,6},{5,7},{6,4},{7,5},{8,10},{9,11},{10,... | collective-permute-start | bytes 21512 | tf_op jit(solution)/shard_map/ppermute | solution.py:46
  4.3 19.3 %collective-permute-start.3 = (bf16[14,256]{1,0:T(8,128)(2,1)S(1)}, bf16[14,256]{1,0:T(8,128)(2,1)S(1)}, u32[]{:S(2)}, u32[]{:S(2)}) collective-permute-start(bf16[14,256]{1,0:T(8,128)(2,1)S(1)} %concatenate.13), channel_id=1, source_target_pairs={{0,1},{1,0},{2,3},{3,2},{4,5},{5,4},{6,7},{7,6},{8,9},{9,8},{10,11... | collective-permute-start | bytes 21512 | tf_op jit(solution)/shard_map/ppermute | solution.py:46
  4.3 20.2 %collective-permute-start.1 = (bf16[128,1024]{1,0:T(8,128)(2,1)}, bf16[128,1024]{1,0:T(8,128)(2,1)S(1)}, u32[]{:S(2)}, u32[]{:S(2)}) collective-permute-start(bf16[128,1024]{1,0:T(8,128)(2,1)} %state.3), channel_id=1, source_target_pairs={{0,2},{1,3},{2,0},{3,1},{4,6},{5,7},{6,4},{7,5},{8,10},{9,11},{10,... | collective-permute-start | bytes 786440 | tf_op jit(solution)/shard_map/ppermute | solution.py:46
  10.5 13.5 %collective-permute-start.8 = (bf16[128,768]{1,0:T(8,128)(2,1)}, bf16[128,768]{1,0:T(8,128)(2,1)S(1)}, u32[]{:S(2)}, u32[]{:S(2)}) collective-permute-start(bf16[128,768]{1,0:T(8,128)(2,1)} %get-tuple-element.136), channel_id=1, source_target_pairs={{0,18},{1,19},{2,16},{3,17},{4,22},{5,23},{6,20},{7,21},{8,26},{9,... | collective-permute-start | bytes 589832 | tf_op jit(solution)/shard_map/ppermute | solution.py:46
  22.4 16.9 %collective-permute-start.6 = (bf16[256,768]{1,0:T(8,128)(2,1)S(1)}, bf16[256,768]{1,0:T(8,128)(2,1)S(1)}, u32[]{:S(2)}, u32[]{:S(2)}) collective-permute-start(bf16[256,768]{1,0:T(8,128)(2,1)S(1)} %copy-done.103), channel_id=1, source_target_pairs={{0,1},{1,0},{2,3},{3,2},{4,5},{5,4},{6,7},{7,6},{8,9},{9,8},{10,11... | collective-permute-start | bytes 1179656 | tf_op jit(solution)/shard_map/ppermute | solution.py:46
  24.0 14.5 %collective-permute-start = (bf16[128,1024]{1,0:T(8,128)(2,1)S(1)}, bf16[128,1024]{1,0:T(8,128)(2,1)S(1)}, u32[]{:S(2)}, u32[]{:S(2)}) collective-permute-start(bf16[128,1024]{1,0:T(8,128)(2,1)S(1)} %copy-done.1), channel_id=1, source_target_pairs={{0,1},{1,0},{2,3},{3,2},{4,5},{5,4},{6,7},{7,6},{8,9},{9,8},{10,11... | collective-permute-start | bytes 786440 | tf_op jit(solution)/shard_map/ppermute | solution.py:46
  24.4 15.7 %collective-permute-start.2 = (bf16[128,1024]{1,0:T(8,128)(2,1)S(1)}, bf16[128,1024]{1,0:T(8,128)(2,1)S(1)}, u32[]{:S(2)}, u32[]{:S(2)}) collective-permute-start(bf16[128,1024]{1,0:T(8,128)(2,1)S(1)} %collective-permute-done.1.x2), channel_id=1, source_target_pairs={{0,1},{1,0},{2,3},{3,2},{4,5},{5,4},{6,7},{7,6},{8,9},{9,8},{10,11... | collective-permute-start | bytes 786440 | tf_op jit(solution)/shard_map/ppermute | solution.py:46
  31.7 21.6 %collective-permute-start.13 = (bf16[256,1024]{1,0:T(8,128)(2,1)}, bf16[256,1024]{1,0:T(8,128)(2,1)S(1)}, u32[]{:S(2)}, u32[]{:S(2)}) collective-permute-start(bf16[256,1024]{1,0:T(8,128)(2,1)} %get-tuple-element.148), channel_id=1, source_target_pairs={{0,1},{1,0},{2,3},{3,2},{4,5},{5,4},{6,7},{7,6},{8,9},{9,8},{10,11... | collective-permute-start | bytes 1572872 | tf_op jit(solution)/shard_map/ppermute | solution.py:46
  38.5 14.0 %collective-permute-start.14 = (bf16[128,1024]{1,0:T(8,128)(2,1)}, bf16[128,1024]{1,0:T(8,128)(2,1)S(1)}, u32[]{:S(2)}, u32[]{:S(2)}) collective-permute-start(bf16[128,1024]{1,0:T(8,128)(2,1)} %get-tuple-element.149), channel_id=1, source_target_pairs={{0,2},{1,3},{2,0},{3,1},{4,6},{5,7},{6,4},{7,5},{8,10},{9,11},{10,... | collective-permute-start | bytes 786440 | tf_op jit(solution)/shard_map/ppermute | solution.py:46
  38.5 14.0 %collective-permute-start.15 = (bf16[128,1024]{1,0:T(8,128)(2,1)}, bf16[128,1024]{1,0:T(8,128)(2,1)S(1)}, u32[]{:S(2)}, u32[]{:S(2)}) collective-permute-start(bf16[128,1024]{1,0:T(8,128)(2,1)} %get-tuple-element.150), channel_id=1, source_target_pairs={{0,18},{1,19},{2,16},{3,17},{4,22},{5,23},{6,20},{7,21},{8,26},{9,... | collective-permute-start | bytes 786440 | tf_op jit(solution)/shard_map/ppermute | solution.py:46
  39.3 13.3 %collective-permute-start.16 = (bf16[128,1024]{1,0:T(8,128)(2,1)}, bf16[128,1024]{1,0:T(8,128)(2,1)S(1)}, u32[]{:S(2)}, u32[]{:S(2)}) collective-permute-start(bf16[128,1024]{1,0:T(8,128)(2,1)} %get-tuple-element.151), channel_id=1, source_target_pairs={{0,3},{1,2},{2,1},{3,0},{4,7},{5,6},{6,5},{7,4},{8,11},{9,10},{10,... | collective-permute-start | bytes 786440 | tf_op jit(solution)/shard_map/ppermute | solution.py:46
  40.1 13.1 %collective-permute-start.17 = (bf16[128,1024]{1,0:T(8,128)(2,1)}, bf16[128,1024]{1,0:T(8,128)(2,1)S(1)}, u32[]{:S(2)}, u32[]{:S(2)}) collective-permute-start(bf16[128,1024]{1,0:T(8,128)(2,1)} %get-tuple-element.152), channel_id=1, source_target_pairs={{0,19},{1,18},{2,17},{3,16},{4,23},{5,22},{6,21},{7,20},{8,27},{9,... | collective-permute-start | bytes 786440 | tf_op jit(solution)/shard_map/ppermute | solution.py:46
  62.9 14.3 %collective-permute-start.12 = (bf16[128,1024]{1,0:T(8,128)(2,1)S(1)}, bf16[128,1024]{1,0:T(8,128)(2,1)S(1)}, u32[]{:S(2)}, u32[]{:S(2)}) collective-permute-start(bf16[128,1024]{1,0:T(8,128)(2,1)S(1)} %add_convert_fusion.5), channel_id=1, source_target_pairs={{0,2},{1,3},{2,0},{3,1},{4,6},{5,7},{6,4},{7,5},{8,10},{9,11},{10,... | collective-permute-start | bytes 786440 | tf_op jit(solution)/shard_map/ppermute | solution.py:46
  64.6 30.0 %collective-permute-start.26 = (bf16[256,1792]{1,0:T(8,128)(2,1)S(1)}, bf16[256,1792]{1,0:T(8,128)(2,1)S(1)}, u32[]{:S(2)}, u32[]{:S(2)}) collective-permute-start(bf16[256,1792]{1,0:T(8,128)(2,1)S(1)} %copy-done.96), channel_id=1, source_target_pairs={{0,1},{1,0},{2,3},{3,2},{4,5},{5,4},{6,7},{7,6},{8,9},{9,8},{10,11... | collective-permute-start | bytes 2752520 | tf_op jit(solution)/shard_map/ppermute | solution.py:46
  64.6 30.0 %collective-permute-start.27 = (bf16[256,1792]{1,0:T(8,128)(2,1)S(1)}, bf16[256,1792]{1,0:T(8,128)(2,1)S(1)}, u32[]{:S(2)}, u32[]{:S(2)}) collective-permute-start(bf16[256,1792]{1,0:T(8,128)(2,1)S(1)} %copy-done.95), channel_id=1, source_target_pairs={{0,18},{1,19},{2,16},{3,17},{4,22},{5,23},{6,20},{7,21},{8,26},{9,... | collective-permute-start | bytes 2752520 | tf_op jit(solution)/shard_map/ppermute | solution.py:46
  65.3 42.6 %collective-permute-start.28 = (bf16[256,1792]{1,0:T(8,128)(2,1)S(1)}, bf16[256,1792]{1,0:T(8,128)(2,1)}, u32[]{:S(2)}, u32[]{:S(2)}) collective-permute-start(bf16[256,1792]{1,0:T(8,128)(2,1)S(1)} %copy-done.94), channel_id=1, source_target_pairs={{0,19},{1,18},{2,17},{3,16},{4,23},{5,22},{6,21},{7,20},{8,27},{9,... | collective-permute-start | bytes 2752520 | tf_op jit(solution)/shard_map/ppermute | solution.py:46
  86.5 21.4 %collective-permute-start.20 = (bf16[128,1024]{1,0:T(8,128)(2,1)}, bf16[128,1024]{1,0:T(8,128)(2,1)S(1)}, u32[]{:S(2)}, u32[]{:S(2)}) collective-permute-start(bf16[128,1024]{1,0:T(8,128)(2,1)} %get-tuple-element.156.n0), channel_id=1, source_target_pairs={{0,1},{1,0},{2,3},{3,2},{4,5},{5,4},{6,7},{7,6},{8,9},{9,8},{10,11... | collective-permute-start | bytes 786440 | tf_op jit(solution)/shard_map/ppermute | solution.py:46
  94.3 13.6 %collective-permute-start.22 = (bf16[128,1024]{1,0:T(8,128)(2,1)S(1)}, bf16[128,1024]{1,0:T(8,128)(2,1)S(1)}, u32[]{:S(2)}, u32[]{:S(2)}) collective-permute-start(bf16[128,1024]{1,0:T(8,128)(2,1)S(1)} %collective-permute-done.21.n2), channel_id=1, source_target_pairs={{0,1},{1,0},{2,3},{3,2},{4,5},{5,4},{6,7},{7,6},{8,9},{9,8},{10,11... | collective-permute-start | bytes 786440 | tf_op jit(solution)/shard_map/ppermute | solution.py:46
  136.4 31.8 %collective-permute-start.68 = (bf16[256,1536]{1,0:T(8,128)(2,1)}, bf16[256,1536]{1,0:T(8,128)(2,1)S(1)}, u32[]{:S(2)}, u32[]{:S(2)}) collective-permute-start(bf16[256,1536]{1,0:T(8,128)(2,1)} %get-tuple-element.218), channel_id=1, source_target_pairs={{0,32},{1,33},{2,34},{3,35},{4,36},{5,37},{6,38},{7,39},{8,40},{9,... | collective-permute-start | bytes 2359304 | tf_op jit(solution)/shard_map/ppermute | solution.py:46
  150.4 19.4 %collective-permute-start.35 = (bf16[128,1024]{1,0:T(8,128)(2,1)}, bf16[128,1024]{1,0:T(8,128)(2,1)S(1)}, u32[]{:S(2)}, u32[]{:S(2)}) collective-permute-start(bf16[128,1024]{1,0:T(8,128)(2,1)} %get-tuple-element.172.u0.up), channel_id=1, source_target_pairs={{0,1},{1,0},{2,3},{3,2},{4,5},{5,4},{6,7},{7,6},{8,9},{9,8},{10,11... | collective-permute-start | bytes 786440 | tf_op jit(solution)/shard_map/ppermute | solution.py:46
  157.7 15.1 %collective-permute-start.37 = (bf16[128,1024]{1,0:T(8,128)(2,1)S(1)}, bf16[128,1024]{1,0:T(8,128)(2,1)S(1)}, u32[]{:S(2)}, u32[]{:S(2)}) collective-permute-start(bf16[128,1024]{1,0:T(8,128)(2,1)S(1)} %collective-permute-done.36.u2), channel_id=1, source_target_pairs={{0,1},{1,0},{2,3},{3,2},{4,5},{5,4},{6,7},{7,6},{8,9},{9,8},{10,11... | collective-permute-start | bytes 786440 | tf_op jit(solution)/shard_map/ppermute | solution.py:46
  157.7 32.4 %collective-permute-start.69 = (bf16[256,1536]{1,0:T(8,128)(2,1)S(1)}, bf16[256,1536]{1,0:T(8,128)(2,1)S(1)}, u32[]{:S(2)}, u32[]{:S(2)}) collective-permute-start(bf16[256,1536]{1,0:T(8,128)(2,1)S(1)} %copy-done.100), channel_id=1, source_target_pairs={{0,64},{1,65},{2,66},{3,67},{4,68},{5,69},{6,70},{7,71},{8,72},{9,... | collective-permute-start | bytes 2359304 | tf_op jit(solution)/shard_map/ppermute | solution.py:46
  160.5 34.6 %collective-permute-start.70 = (bf16[256,1536]{1,0:T(8,128)(2,1)S(1)}, bf16[256,1536]{1,0:T(8,128)(2,1)S(1)}, u32[]{:S(2)}, u32[]{:S(2)}) collective-permute-start(bf16[256,1536]{1,0:T(8,128)(2,1)S(1)} %copy-done.99), channel_id=1, source_target_pairs={{0,96},{1,97},{2,98},{3,99},{4,100},{5,101},{6,102},{7,103},{8,104... | collective-permute-start | bytes 2359304 | tf_op jit(solution)/shard_map/ppermute | solution.py:46
  168.2 35.3 %collective-permute-start.74 = (bf16[256,1536]{1,0:T(8,128)(2,1)}, bf16[256,1536]{1,0:T(8,128)(2,1)S(1)}, u32[]{:S(2)}, u32[]{:S(2)}) collective-permute-start(bf16[256,1536]{1,0:T(8,128)(2,1)} %get-tuple-element.227), channel_id=1, source_target_pairs={{0,4},{1,5},{2,6},{3,7},{4,8},{5,9},{6,10},{7,11},{8,12},{9,13},{1... | collective-permute-start | bytes 2359304 | tf_op jit(solution)/shard_map/ppermute | solution.py:46
  169.9 38.4 %collective-permute-start.75 = (bf16[256,1536]{1,0:T(8,128)(2,1)}, bf16[256,1536]{1,0:T(8,128)(2,1)S(1)}, u32[]{:S(2)}, u32[]{:S(2)}) collective-permute-start(bf16[256,1536]{1,0:T(8,128)(2,1)} %get-tuple-element.228), channel_id=1, source_target_pairs={{0,8},{1,9},{2,10},{3,11},{4,12},{5,13},{6,14},{7,15},{8,0},{9,1},... | collective-permute-start | bytes 2359304 | tf_op jit(solution)/shard_map/ppermute | solution.py:46
  172.8 35.5 %collective-permute-start.76 = (bf16[256,1536]{1,0:T(8,128)(2,1)}, bf16[256,1536]{1,0:T(8,128)(2,1)S(1)}, u32[]{:S(2)}, u32[]{:S(2)}) collective-permute-start(bf16[256,1536]{1,0:T(8,128)(2,1)} %get-tuple-element.229), channel_id=1, source_target_pairs={{0,12},{1,13},{2,14},{3,15},{4,0},{5,1},{6,2},{7,3},{8,4},{9,5},{1... | collective-permute-start | bytes 2359304 | tf_op jit(solution)/shard_map/ppermute | solution.py:46
  199.0 14.4 %collective-permute-start.71 = (bf16[64,1536]{1,0:T(8,128)(2,1)}, bf16[64,1536]{1,0:T(8,128)(2,1)S(1)}, u32[]{:S(2)}, u32[]{:S(2)}) collective-permute-start(bf16[64,1536]{1,0:T(8,128)(2,1)} %get-tuple-element.222), channel_id=1, source_target_pairs={{0,4},{1,5},{2,6},{3,7},{4,8},{5,9},{6,10},{7,11},{8,12},{9,13},{1... | collective-permute-start | bytes 589832 | tf_op jit(solution)/shard_map/ppermute | solution.py:46
  200.6 22.0 %collective-permute-start.72 = (bf16[64,1536]{1,0:T(8,128)(2,1)}, bf16[64,1536]{1,0:T(8,128)(2,1)S(1)}, u32[]{:S(2)}, u32[]{:S(2)}) collective-permute-start(bf16[64,1536]{1,0:T(8,128)(2,1)} %get-tuple-element.223), channel_id=1, source_target_pairs={{0,8},{1,9},{2,10},{3,11},{4,12},{5,13},{6,14},{7,15},{8,0},{9,1},... | collective-permute-start | bytes 589832 | tf_op jit(solution)/shard_map/ppermute | solution.py:46
  203.5 20.0 %collective-permute-start.73 = (bf16[64,1536]{1,0:T(8,128)(2,1)}, bf16[64,1536]{1,0:T(8,128)(2,1)S(1)}, u32[]{:S(2)}, u32[]{:S(2)}) collective-permute-start(bf16[64,1536]{1,0:T(8,128)(2,1)} %get-tuple-element.224), channel_id=1, source_target_pairs={{0,12},{1,13},{2,14},{3,15},{4,0},{5,1},{6,2},{7,3},{8,4},{9,5},{1... | collective-permute-start | bytes 589832 | tf_op jit(solution)/shard_map/ppermute | solution.py:46
  222.6 36.1 %collective-permute-start.40 = (bf16[256,1536]{1,0:T(8,128)(2,1)}, bf16[256,1536]{1,0:T(8,128)(2,1)S(1)}, u32[]{:S(2)}, u32[]{:S(2)}) collective-permute-start(bf16[256,1536]{1,0:T(8,128)(2,1)} %get-tuple-element.182), channel_id=1, source_target_pairs={{0,32},{1,33},{2,34},{3,35},{4,36},{5,37},{6,38},{7,39},{8,40},{9,... | collective-permute-start | bytes 2359304 | tf_op jit(solution)/shard_map/ppermute | solution.py:46
  223.5 23.8 %collective-permute-start.29 = (bf16[256,1024]{1,0:T(8,128)(2,1)S(1)}, bf16[256,1024]{1,0:T(8,128)(2,1)S(1)}, u32[]{:S(2)}, u32[]{:S(2)}) collective-permute-start(bf16[256,1024]{1,0:T(8,128)(2,1)S(1)} %copy-done.101), channel_id=1, source_target_pairs={{0,1},{1,0},{2,3},{3,2},{4,5},{5,4},{6,7},{7,6},{8,9},{9,8},{10,11... | collective-permute-start | bytes 1572872 | tf_op jit(solution)/shard_map/ppermute | solution.py:46
  227.8 14.8 %collective-permute-start.82 = (bf16[32,4864]{1,0:T(8,128)(2,1)}, bf16[32,4864]{1,0:T(8,128)(2,1)S(1)}, u32[]{:S(2)}, u32[]{:S(2)}) collective-permute-start(bf16[32,4864]{1,0:T(8,128)(2,1)} %get-tuple-element.237), channel_id=1, source_target_pairs={{0,16},{1,17},{2,18},{3,19},{4,20},{5,21},{6,22},{7,23},{8,24},{9,... | collective-permute-start | bytes 933896 | tf_op jit(solution)/shard_map/ppermute | solution.py:46
  234.8 27.0 %collective-permute-start.41 = (bf16[256,1536]{1,0:T(8,128)(2,1)}, bf16[256,1536]{1,0:T(8,128)(2,1)S(1)}, u32[]{:S(2)}, u32[]{:S(2)}) collective-permute-start(bf16[256,1536]{1,0:T(8,128)(2,1)} %get-tuple-element.183), channel_id=1, source_target_pairs={{0,64},{1,65},{2,66},{3,67},{4,68},{5,69},{6,70},{7,71},{8,72},{9,... | collective-permute-start | bytes 2359304 | tf_op jit(solution)/shard_map/ppermute | solution.py:46
  236.9 16.9 %collective-permute-start.38 = (bf16[256,1024]{1,0:T(8,128)(2,1)S(1)}, bf16[256,1024]{1,0:T(8,128)(2,1)S(1)}, u32[]{:S(2)}, u32[]{:S(2)}) collective-permute-start(bf16[256,1024]{1,0:T(8,128)(2,1)S(1)} %copy-done.102), channel_id=1, source_target_pairs={{0,1},{1,0},{2,3},{3,2},{4,5},{5,4},{6,7},{7,6},{8,9},{9,8},{10,11... | collective-permute-start | bytes 1572872 | tf_op jit(solution)/shard_map/ppermute | solution.py:46
  242.7 29.7 %collective-permute-start.42 = (bf16[256,1536]{1,0:T(8,128)(2,1)}, bf16[256,1536]{1,0:T(8,128)(2,1)S(1)}, u32[]{:S(2)}, u32[]{:S(2)}) collective-permute-start(bf16[256,1536]{1,0:T(8,128)(2,1)} %get-tuple-element.184), channel_id=1, source_target_pairs={{0,96},{1,97},{2,98},{3,99},{4,100},{5,101},{6,102},{7,103},{8,104... | collective-permute-start | bytes 2359304 | tf_op jit(solution)/shard_map/ppermute | solution.py:46
  253.8 28.6 %collective-permute-start.46 = (bf16[256,1536]{1,0:T(8,128)(2,1)}, bf16[256,1536]{1,0:T(8,128)(2,1)S(1)}, u32[]{:S(2)}, u32[]{:S(2)}) collective-permute-start(bf16[256,1536]{1,0:T(8,128)(2,1)} %get-tuple-element.191), channel_id=1, source_target_pairs={{0,4},{1,5},{2,6},{3,7},{4,8},{5,9},{6,10},{7,11},{8,12},{9,13},{1... | collective-permute-start | bytes 2359304 | tf_op jit(solution)/shard_map/ppermute | solution.py:46
  257.7 35.9 %collective-permute-start.47 = (bf16[256,1536]{1,0:T(8,128)(2,1)}, bf16[256,1536]{1,0:T(8,128)(2,1)S(1)}, u32[]{:S(2)}, u32[]{:S(2)}) collective-permute-start(bf16[256,1536]{1,0:T(8,128)(2,1)} %get-tuple-element.192), channel_id=1, source_target_pairs={{0,8},{1,9},{2,10},{3,11},{4,12},{5,13},{6,14},{7,15},{8,0},{9,1},... | collective-permute-start | bytes 2359304 | tf_op jit(solution)/shard_map/ppermute | solution.py:46
  258.8 34.9 %collective-permute-start.48 = (bf16[256,1536]{1,0:T(8,128)(2,1)}, bf16[256,1536]{1,0:T(8,128)(2,1)}, u32[]{:S(2)}, u32[]{:S(2)}) collective-permute-start(bf16[256,1536]{1,0:T(8,128)(2,1)} %get-tuple-element.193), channel_id=1, source_target_pairs={{0,12},{1,13},{2,14},{3,15},{4,0},{5,1},{6,2},{7,3},{8,4},{9,5},{1... | collective-permute-start | bytes 2359304 | tf_op jit(solution)/shard_map/ppermute | solution.py:46
  261.8 15.9 %collective-permute-start.31 = (bf16[256,1024]{1,0:T(8,128)(2,1)}, bf16[256,1024]{1,0:T(8,128)(2,1)S(1)}, u32[]{:S(2)}, u32[]{:S(2)}) collective-permute-start(bf16[256,1024]{1,0:T(8,128)(2,1)} %get-tuple-element.167), channel_id=1, source_target_pairs={{0,1},{1,0},{2,3},{3,2},{4,5},{5,4},{6,7},{7,6},{8,9},{9,8},{10,11... | collective-permute-start | bytes 1572872 | tf_op jit(solution)/shard_map/ppermute | solution.py:46
  277.7 22.7 %collective-permute-start.92 = (bf16[64,1536]{1,0:T(8,128)(2,1)S(1)}, bf16[64,1536]{1,0:T(8,128)(2,1)S(1)}, u32[]{:S(2)}, u32[]{:S(2)}) collective-permute-start(bf16[64,1536]{1,0:T(8,128)(2,1)S(1)} %copy-done.64), channel_id=1, source_target_pairs={{0,32},{1,33},{2,34},{3,35},{4,36},{5,37},{6,38},{7,39},{8,40},{9,... | collective-permute-start | bytes 589832 | tf_op jit(solution)/shard_map/ppermute | solution.py:46
  279.9 20.9 %collective-permute-start.91 = (bf16[64,1536]{1,0:T(8,128)(2,1)S(1)}, bf16[64,1536]{1,0:T(8,128)(2,1)S(1)}, u32[]{:S(2)}, u32[]{:S(2)}) collective-permute-start(bf16[64,1536]{1,0:T(8,128)(2,1)S(1)} %copy-done.64), channel_id=1, source_target_pairs={{0,64},{1,65},{2,66},{3,67},{4,68},{5,69},{6,70},{7,71},{8,72},{9,... | collective-permute-start | bytes 589832 | tf_op jit(solution)/shard_map/ppermute | solution.py:46
  282.5 20.3 %collective-permute-start.90 = (bf16[64,1536]{1,0:T(8,128)(2,1)S(1)}, bf16[64,1536]{1,0:T(8,128)(2,1)S(1)}, u32[]{:S(2)}, u32[]{:S(2)}) collective-permute-start(bf16[64,1536]{1,0:T(8,128)(2,1)S(1)} %copy-done.64), channel_id=1, source_target_pairs={{0,96},{1,97},{2,98},{3,99},{4,100},{5,101},{6,102},{7,103},{8,104... | collective-permute-start | bytes 589832 | tf_op jit(solution)/shard_map/ppermute | solution.py:46
  300.4 25.5 %collective-permute-start.30 = (bf16[128,1024]{1,0:T(8,128)(2,1)S(1)}, bf16[128,1024]{1,0:T(8,128)(2,1)S(1)}, u32[]{:S(2)}, u32[]{:S(2)}) collective-permute-start(bf16[128,1024]{1,0:T(8,128)(2,1)S(1)} %add_convert_fusion.3), channel_id=1, source_target_pairs={{0,2},{1,3},{2,0},{3,1},{4,6},{5,7},{6,4},{7,5},{8,10},{9,11},{10,... | collective-permute-start | bytes 786440 | tf_op jit(solution)/shard_map/ppermute | solution.py:46
  305.8 14.8 %collective-permute-start.51 = (bf16[64,1536]{1,0:T(8,128)(2,1)}, bf16[64,1536]{1,0:T(8,128)(2,1)S(1)}, u32[]{:S(2)}, u32[]{:S(2)}) collective-permute-start(bf16[64,1536]{1,0:T(8,128)(2,1)} %get-tuple-element.197), channel_id=1, source_target_pairs={{0,96},{1,97},{2,98},{3,99},{4,100},{5,101},{6,102},{7,103},{8,104... | collective-permute-start | bytes 589832 | tf_op jit(solution)/shard_map/ppermute | solution.py:46
  307.2 21.2 %collective-permute-start.32 = (bf16[128,1024]{1,0:T(8,128)(2,1)S(1)}, bf16[128,1024]{1,0:T(8,128)(2,1)S(1)}, u32[]{:S(2)}, u32[]{:S(2)}) collective-permute-start(bf16[128,1024]{1,0:T(8,128)(2,1)S(1)} %add_convert_fusion.2), channel_id=1, source_target_pairs={{0,2},{1,3},{2,0},{3,1},{4,6},{5,7},{6,4},{7,5},{8,10},{9,11},{10,... | collective-permute-start | bytes 786440 | tf_op jit(solution)/shard_map/ppermute | solution.py:46
  314.0 43.1 %collective-permute-start.95 = (bf16[256,1536]{1,0:T(8,128)(2,1)}, bf16[256,1536]{1,0:T(8,128)(2,1)S(1)}, u32[]{:S(2)}, u32[]{:S(2)}) collective-permute-start(bf16[256,1536]{1,0:T(8,128)(2,1)} %shard_map.256.refs_4_), channel_id=1, source_target_pairs={{0,4},{1,5},{2,6},{3,7},{4,8},{5,9},{6,10},{7,11},{8,12},{9,13},{1... | collective-permute-start | bytes 2359304 | tf_op jit(solution)/shard_map/ppermute | solution.py:46
  314.6 43.9 %collective-permute-start.94 = (bf16[256,1536]{1,0:T(8,128)(2,1)}, bf16[256,1536]{1,0:T(8,128)(2,1)S(1)}, u32[]{:S(2)}, u32[]{:S(2)}) collective-permute-start(bf16[256,1536]{1,0:T(8,128)(2,1)} %shard_map.256.refs_4_), channel_id=1, source_target_pairs={{0,8},{1,9},{2,10},{3,11},{4,12},{5,13},{6,14},{7,15},{8,0},{9,1},... | collective-permute-start | bytes 2359304 | tf_op jit(solution)/shard_map/ppermute | solution.py:46
  334.5 21.5 %collective-permute-start.86 = (bf16[64,1536]{1,0:T(8,128)(2,1)S(1)}, bf16[64,1536]{1,0:T(8,128)(2,1)S(1)}, u32[]{:S(2)}, u32[]{:S(2)}) collective-permute-start(bf16[64,1536]{1,0:T(8,128)(2,1)S(1)} %copy-done.62), channel_id=1, source_target_pairs={{0,4},{1,5},{2,6},{3,7},{4,8},{5,9},{6,10},{7,11},{8,12},{9,13},{1... | collective-permute-start | bytes 589832 | tf_op jit(solution)/shard_map/ppermute | solution.py:46
  343.3 12.7 %collective-permute-start.85 = (bf16[64,1536]{1,0:T(8,128)(2,1)S(1)}, bf16[64,1536]{1,0:T(8,128)(2,1)S(1)}, u32[]{:S(2)}, u32[]{:S(2)}) collective-permute-start(bf16[64,1536]{1,0:T(8,128)(2,1)S(1)} %copy-done.62), channel_id=1, source_target_pairs={{0,8},{1,9},{2,10},{3,11},{4,12},{5,13},{6,14},{7,15},{8,0},{9,1},... | collective-permute-start | bytes 589832 | tf_op jit(solution)/shard_map/ppermute | solution.py:46
  356.0 18.6 %collective-permute-start.58 = (bf16[80,1536]{1,0:T(8,128)(2,1)}, bf16[80,1536]{1,0:T(8,128)(2,1)S(1)}, u32[]{:S(2)}, u32[]{:S(2)}) collective-permute-start(bf16[80,1536]{1,0:T(8,128)(2,1)} %get-tuple-element.210.own), channel_id=1, source_target_pairs={{0,4},{1,5},{2,6},{3,7},{4,8},{5,9},{6,10},{7,11},{8,12},{9,13},{1... | collective-permute-start | bytes 737288 | tf_op jit(solution)/shard_map/ppermute | solution.py:46
  356.1 14.5 %collective-permute-start.63 = (bf16[64,1536]{1,0:T(8,128)(2,1)}, bf16[64,1536]{1,0:T(8,128)(2,1)S(1)}, u32[]{:S(2)}, u32[]{:S(2)}) collective-permute-start(bf16[64,1536]{1,0:T(8,128)(2,1)} %get-tuple-element.211.own), channel_id=1, source_target_pairs={{0,64},{1,65},{2,66},{3,67},{4,68},{5,69},{6,70},{7,71},{8,72},{9,... | collective-permute-start | bytes 589832 | tf_op jit(solution)/shard_map/ppermute | solution.py:46
  357.1 22.6 %collective-permute-start.57 = (bf16[80,1536]{1,0:T(8,128)(2,1)}, bf16[80,1536]{1,0:T(8,128)(2,1)S(1)}, u32[]{:S(2)}, u32[]{:S(2)}) collective-permute-start(bf16[80,1536]{1,0:T(8,128)(2,1)} %get-tuple-element.210.own), channel_id=1, source_target_pairs={{0,8},{1,9},{2,10},{3,11},{4,12},{5,13},{6,14},{7,15},{8,0},{9,1},... | collective-permute-start | bytes 737288 | tf_op jit(solution)/shard_map/ppermute | solution.py:46
  358.5 21.6 %collective-permute-start.56 = (bf16[80,1536]{1,0:T(8,128)(2,1)}, bf16[80,1536]{1,0:T(8,128)(2,1)S(1)}, u32[]{:S(2)}, u32[]{:S(2)}) collective-permute-start(bf16[80,1536]{1,0:T(8,128)(2,1)} %get-tuple-element.210.own), channel_id=1, source_target_pairs={{0,12},{1,13},{2,14},{3,15},{4,0},{5,1},{6,2},{7,3},{8,4},{9,5},{1... | collective-permute-start | bytes 737288 | tf_op jit(solution)/shard_map/ppermute | solution.py:46
  370.6 18.8 %collective-permute-start.93 = (bf16[256,1536]{1,0:T(8,128)(2,1)S(1)}, bf16[256,1536]{1,0:T(8,128)(2,1)S(1)}, u32[]{:S(2)}, u32[]{:S(2)}) collective-permute-start(bf16[256,1536]{1,0:T(8,128)(2,1)S(1)} %copy-done), channel_id=1, source_target_pairs={{0,12},{1,13},{2,14},{3,15},{4,0},{5,1},{6,2},{7,3},{8,4},{9,5},{1... | collective-permute-start | bytes 2359304 | tf_op jit(solution)/shard_map/ppermute | solution.py:46
  374.6 37.8 %collective-permute-start.89 = (bf16[256,1536]{1,0:T(8,128)(2,1)}, bf16[256,1536]{1,0:T(8,128)(2,1)S(1)}, u32[]{:S(2)}, u32[]{:S(2)}) collective-permute-start(bf16[256,1536]{1,0:T(8,128)(2,1)} %shard_map.255.refs_0_), channel_id=1, source_target_pairs={{0,32},{1,33},{2,34},{3,35},{4,36},{5,37},{6,38},{7,39},{8,40},{9,... | collective-permute-start | bytes 2359304 | tf_op jit(solution)/shard_map/ppermute | solution.py:46
  374.6 38.5 %collective-permute-start.88 = (bf16[256,1536]{1,0:T(8,128)(2,1)}, bf16[256,1536]{1,0:T(8,128)(2,1)S(1)}, u32[]{:S(2)}, u32[]{:S(2)}) collective-permute-start(bf16[256,1536]{1,0:T(8,128)(2,1)} %shard_map.255.refs_0_), channel_id=1, source_target_pairs={{0,64},{1,65},{2,66},{3,67},{4,68},{5,69},{6,70},{7,71},{8,72},{9,... | collective-permute-start | bytes 2359304 | tf_op jit(solution)/shard_map/ppermute | solution.py:46
  379.7 34.6 %collective-permute-start.87 = (bf16[256,1536]{1,0:T(8,128)(2,1)}, bf16[256,1536]{1,0:T(8,128)(2,1)}, u32[]{:S(2)}, u32[]{:S(2)}) collective-permute-start(bf16[256,1536]{1,0:T(8,128)(2,1)} %shard_map.255.refs_0_), channel_id=1, source_target_pairs={{0,96},{1,97},{2,98},{3,99},{4,100},{5,101},{6,102},{7,103},{8,104... | collective-permute-start | bytes 2359304 | tf_op jit(solution)/shard_map/ppermute | solution.py:46
  380.1 34.3 %collective-permute-start.67 = (bf16[256,1536]{1,0:T(8,128)(2,1)}, bf16[256,1536]{1,0:T(8,128)(2,1)}, u32[]{:S(2)}, u32[]{:S(2)}) collective-permute-start(bf16[256,1536]{1,0:T(8,128)(2,1)} %shard_map.247.refs_4_), channel_id=1, source_target_pairs={{0,4},{1,5},{2,6},{3,7},{4,8},{5,9},{6,10},{7,11},{8,12},{9,13},{1... | collective-permute-start | bytes 2359304 | tf_op jit(solution)/shard_map/ppermute | solution.py:46
  389.4 56.2 %collective-permute-start.61 = (bf16[272,1536]{1,0:T(8,128)(2,1)}, bf16[272,1536]{1,0:T(8,128)(2,1)S(1)}, u32[]{:S(2)}, u32[]{:S(2)}) collective-permute-start(bf16[272,1536]{1,0:T(8,128)(2,1)} %shard_map.246.refs_0_), channel_id=1, source_target_pairs={{0,32},{1,33},{2,34},{3,35},{4,36},{5,37},{6,38},{7,39},{8,40},{9,... | collective-permute-start | bytes 2506760 | tf_op jit(solution)/shard_map/ppermute | solution.py:46
  412.4 34.1 %collective-permute-start.60 = (bf16[272,1536]{1,0:T(8,128)(2,1)}, bf16[272,1536]{1,0:T(8,128)(2,1)S(1)}, u32[]{:S(2)}, u32[]{:S(2)}) collective-permute-start(bf16[272,1536]{1,0:T(8,128)(2,1)} %shard_map.246.refs_0_), channel_id=1, source_target_pairs={{0,64},{1,65},{2,66},{3,67},{4,68},{5,69},{6,70},{7,71},{8,72},{9,... | collective-permute-start | bytes 2506760 | tf_op jit(solution)/shard_map/ppermute | solution.py:46
  413.1 34.0 %collective-permute-start.59 = (bf16[272,1536]{1,0:T(8,128)(2,1)}, bf16[272,1536]{1,0:T(8,128)(2,1)S(1)}, u32[]{:S(2)}, u32[]{:S(2)}) collective-permute-start(bf16[272,1536]{1,0:T(8,128)(2,1)} %shard_map.246.refs_0_), channel_id=1, source_target_pairs={{0,96},{1,97},{2,98},{3,99},{4,100},{5,101},{6,102},{7,103},{8,104... | collective-permute-start | bytes 2506760 | tf_op jit(solution)/shard_map/ppermute | solution.py:46
  414.4 19.5 %collective-permute-start.66 = (bf16[256,1536]{1,0:T(8,128)(2,1)}, bf16[256,1536]{1,0:T(8,128)(2,1)S(1)}, u32[]{:S(2)}, u32[]{:S(2)}) collective-permute-start(bf16[256,1536]{1,0:T(8,128)(2,1)} %shard_map.247.refs_4_), channel_id=1, source_target_pairs={{0,8},{1,9},{2,10},{3,11},{4,12},{5,13},{6,14},{7,15},{8,0},{9,1},... | collective-permute-start | bytes 2359304 | tf_op jit(solution)/shard_map/ppermute | solution.py:46
  414.4 31.2 %collective-permute-start.65 = (bf16[256,1536]{1,0:T(8,128)(2,1)}, bf16[256,1536]{1,0:T(8,128)(2,1)S(1)}, u32[]{:S(2)}, u32[]{:S(2)}) collective-permute-start(bf16[256,1536]{1,0:T(8,128)(2,1)} %shard_map.247.refs_4_), channel_id=1, source_target_pairs={{0,12},{1,13},{2,14},{3,15},{4,0},{5,1},{6,2},{7,3},{8,4},{9,5},{1... | collective-permute-start | bytes 2359304 | tf_op jit(solution)/shard_map/ppermute | solution.py:46
  (148 other events, 1371.6 us)
